TPU v7x, 256 devices: a whole 4x4x8 slice. The times are simulated.
256 devices in a mesh: row: 8 (over z), col: 32 (over y, x, core).
Axes of the slice: x: 4, y: 4, z: 8, core: 2. Of those that a mesh axis runs over, the one named last changes fastest.
Arguments:
- right_side: float32 [4, 8192, 256], P(None, ('row', 'col')), may hold values from -6 to 6
- diag_blocks: bfloat16 [4, 4, 8192, 256], P(None, None, ('row', 'col')), may hold values from -1.2 to 4, as said below
- lower_blocks: bfloat16 [4, 4, 8192, 256], P(None, None, ('row', 'col')), may hold values from -2.390625 to 2.390625
- upper_blocks: bfloat16 [4, 4, 8192, 256], P(None, None, ('row', 'col')), may hold values from -2.390625 to 2.390625
- precond: bfloat16 [4, 4, 8192, 256], P(None, None, ('row', 'col')), may hold values from -0.2 to 0.5, as said below
- junction_out: float32 [2, 4, 4, 8192], P(None, None, None, ('row', 'col')), may hold values from -3 to 3
- junction_in: float32 [2, 4, 4, 8192], P(None, None, None, ('row', 'col')), may hold values from -3 to 3
- end_junction: int32 [2, 8192], P(None, ('row', 'col')), may hold values from 0 to 1023, as said below
- pipe_length: int32 [8192], P(('row', 'col')), may hold values from 1 to 256, 1310720 in all
Outputs:
- adjoint: float32 [4, 8192, 256], P(None, ('row', 'col'))
Inputs may be any that keep to these rules, and one draw needn't show every extreme that they name: The owner column end_junction // 32 lies within 2 columns of the pipe's own mesh column, counted cyclically over the row's columns, and distance 2 occurs on both sides. `diag_blocks`: diagonally dominant: diagonal entries 2 to 4, others at most 1.2 in magnitude. `precond`: diagonal entries 0.2 to 0.5, others at most 0.2 in magnitude.
All inputs are finite; a program needn't handle non-finite values. No bound on the sum of `pipe_length` on one device may be relied on, other than what follows from the above.
Results may differ from a plain program's by a relative error of at most 0.0003.
Values sent between devices are 32-bit elements; how exact they have to be, the bound alone decides.
A program may use at most 64 MiB of HBM per device.

v0:
```python
import jax
import jax.numpy as jnp
from jax import lax
from jax.sharding import PartitionSpec as P

ITERS = 4
REACH = 2


def from_behind(value, axis, steps):
    count = lax.axis_size(axis)
    pairs = [(source, (source + steps) % count) for source in range(count)]
    return lax.ppermute(value, axis, pairs)


def block_transpose(blocks, vec):
    out = blocks[0].astype(jnp.float32) * vec[0]
    for index in range(1, 4):
        out = out + blocks[index].astype(jnp.float32) * vec[index]
    return out


def block_apply(blocks, vec):
    out = blocks[:, 0].astype(jnp.float32) * vec[0]
    for index in range(1, 4):
        out = out + blocks[:, index].astype(jnp.float32) * vec[index]
    return out


def least_squares(hess, beta, steps):
    upper = [list(line) for line in hess]
    target = [beta] + [jnp.float32(0.0) * beta for i in range(steps)]
    cosines = []
    sines = []
    for k in range(steps):
        for i in range(k):
            temp = cosines[i] * upper[i][k] + sines[i] * upper[i + 1][k]
            upper[i + 1][k] = -sines[i] * upper[i][k] + cosines[i] * upper[i + 1][k]
            upper[i][k] = temp
        radius = jnp.sqrt(upper[k][k] * upper[k][k] + upper[k + 1][k] * upper[k + 1][k])
        cosines.append(upper[k][k] / radius)
        sines.append(upper[k + 1][k] / radius)
        upper[k][k] = radius
        target[k + 1] = -sines[k] * target[k]
        target[k] = cosines[k] * target[k]
    coeffs = [None] * steps
    for k in range(steps - 1, -1, -1):
        total = target[k]
        for j in range(k + 1, steps):
            total = total - upper[k][j] * coeffs[j]
        coeffs[k] = total / upper[k][k]
    return coeffs


def local_partials(contrib, end_junction):
    owned_count = contrib.shape[2]
    columns = lax.axis_size("col")
    own_column = lax.axis_index("col")
    owner = end_junction // owned_count
    distance = (owner - own_column + REACH) % columns - REACH
    slot = (distance + REACH) * owned_count + end_junction % owned_count
    flat = jnp.transpose(contrib, (1, 0, 2)).reshape(4, -1)
    partial_value = (
        jnp.zeros((4, (2 * REACH + 1) * owned_count), jnp.float32).at[:, slot.reshape(-1)].add(flat)
    )
    return (partial_value, slot, owned_count)


def junction_near(contrib, end_junction):
    partial_value, slot, owned_count = local_partials(contrib, end_junction)
    owned = partial_value[:, REACH * owned_count : (REACH + 1) * owned_count]
    for offset in range(-REACH, REACH + 1):
        if offset != 0:
            piece = partial_value[
                :, (offset + REACH) * owned_count : (offset + REACH + 1) * owned_count
            ]
            owned = owned + from_behind(piece, "col", offset)
    pieces = []
    for offset in range(-REACH, REACH + 1):
        if offset == 0:
            pieces.append(owned)
        else:
            pieces.append(from_behind(owned, "col", -offset))
    full = jnp.concatenate(pieces, axis=1)
    return jnp.transpose(full[:, slot], (1, 0, 2))


def global_sum(value):
    return lax.psum(value, ("row", "col"))


def body(
    right_side,
    diag_blocks,
    lower_blocks,
    upper_blocks,
    precond,
    junction_out,
    junction_in,
    end_junction,
    pipe_length,
):
    seg_count = right_side.shape[2]
    slots = jnp.arange(seg_count, dtype=jnp.int32)
    active = (slots[None, :] < pipe_length[:, None]).astype(jnp.float32)
    last_slot = pipe_length - 1
    start = active[None] * right_side
    beta = jnp.sqrt(global_sum(jnp.sum(start * start)))
    basis = [start / beta]
    hess = [[jnp.float32(0.0) for col in range(ITERS)] for line in range(ITERS + 1)]
    for step in range(ITERS):
        vec = block_apply(precond, basis[step])
        diag_part = block_transpose(diag_blocks, vec)
        lower = block_transpose(lower_blocks, vec)
        upper = block_transpose(upper_blocks, vec)
        zeros = jnp.zeros_like(lower[:, :, :1])
        following = jnp.concatenate([lower[:, :, 1:], zeros], axis=2)
        preceding = jnp.concatenate([zeros, upper[:, :, :-1]], axis=2)
        first = vec[:, :, 0]
        last = jnp.take_along_axis(vec, last_slot[None, :, None], axis=2)[:, :, 0]
        ends = jnp.stack([first, last])
        contrib = jnp.sum(junction_out * ends[:, :, None, :], axis=1)
        back = junction_near(contrib, end_junction)
        added = jnp.sum(junction_in * back[:, :, None, :], axis=1)
        at_first = jnp.where(slots[None, None, :] == 0, added[0][:, :, None], 0.0)
        at_last = jnp.where(
            slots[None, None, :] == last_slot[None, :, None], added[1][:, :, None], 0.0
        )
        work = active[None] * (diag_part + following + preceding + at_first + at_last)
        for i in range(step + 1):
            product = lax.psum(jnp.sum(basis[i] * work), ("row", "col"))
            work = work - product * basis[i]
            hess[i][step] = product
        size = jnp.sqrt(global_sum(jnp.sum(work * work)))
        hess[step + 1][step] = size
        basis.append(work / size)
    coeffs = least_squares(hess, beta, ITERS)
    combined = coeffs[0] * basis[0]
    for step in range(1, ITERS):
        combined = combined + coeffs[step] * basis[step]
    return block_apply(precond, combined)


def solution(mesh):
    in_specs = (
        P(None, ("row", "col"), None),
        P(None, None, ("row", "col"), None),
        P(None, None, ("row", "col"), None),
        P(None, None, ("row", "col"), None),
        P(None, None, ("row", "col"), None),
        P(None, None, None, ("row", "col")),
        P(None, None, None, ("row", "col")),
        P(None, ("row", "col")),
        P(("row", "col")),
    )
    out_specs = P(None, ("row", "col"), None)
    return jax.shard_map(body, mesh=mesh, in_specs=in_specs, out_specs=out_specs, check_vma=False)
```

profile of v0, /device:TPU:1, one launch (start us, length us, event | category | flops | bytes accessed | tf_op | source)
XLA Modules:
  0.0 1431.1 jit_solution(6159771319336542307)
XLA Ops:
  4.4 81.4 %psum.105 = f32[]{:T(128)} all-reduce(f32[]{:T(128)} %multiply_reduce_fusion.14), channel_id=1, replica_groups=mesh['row'=8,'col'=32] {'row','col'}, use_global_device_ids=true, to_apply=%region_1.0 | all-reduce | flops 1 | bytes 8 | tf_op jit(solution)/shard_map/psum | solution.py:89
  89.5 1.8 copy.135
  91.3 1.9 copy.137
  93.2 1.8 copy.136
  95.0 7.8 fusion.2
  102.8 1.9 copy-done
  111.0 14.6 %slice_reduce_fusion.15 = (f32[32,256]{1,0:T(8,128)S(1)}, f32[32,256]{1,0:T(8,128)S(1)}, f32[32,256]{1,0:T(8,128)S(1)}, f32[32,256]{1,0:T(8,128)}) fusion(f32[4,32,256]{0,2,1:T(8,128)} %copy-done), kind=kLoop, calls=%fused_computation.62 | loop fusion | bytes 262144 | tf_op jit(solution)/shard_map/slice | solution.py:17
  132.5 4.3 collective-permute-start.7
  136.8 6.0 collective-permute-start.6
  146.3 2.1 gather_fusion
  150.6 2.3 multiply_reduce_fusion.13
  152.9 75.8 %psum.106 = f32[]{:T(128)} all-reduce(f32[]{:T(128)} %get-tuple-element.34), channel_id=1, replica_groups=mesh['row'=8,'col'=32] {'row','col'}, use_global_device_ids=true, to_apply=%region_6.8 | all-reduce | flops 1 | bytes 8 | tf_op jit(solution)/shard_map/psum | solution.py:131
  228.8 2.2 multiply_reduce_fusion.12
  230.9 74.3 %psum.107 = f32[]{:T(128)} all-reduce(f32[]{:T(128)} %multiply_reduce_fusion.12), channel_id=1, replica_groups=mesh['row'=8,'col'=32] {'row','col'}, use_global_device_ids=true, to_apply=%region_8.10 | all-reduce | flops 1 | bytes 8 | tf_op jit(solution)/shard_map/psum | solution.py:89
  306.0 1.6 broadcast_divide_fusion.2
  307.5 7.8 fusion.5
  315.3 1.9 copy-done.1
  317.9 2.0 gather_fusion.5
  319.8 14.6 %slice_reduce_fusion.11 = (f32[32,256]{1,0:T(8,128)S(1)}, f32[32,256]{1,0:T(8,128)S(1)}, f32[32,256]{1,0:T(8,128)S(1)}, f32[32,256]{1,0:T(8,128)}) fusion(f32[4,32,256]{0,2,1:T(8,128)} %copy-done.1), kind=kLoop, calls=%fused_computation.58 | loop fusion | bytes 262144 | tf_op jit(solution)/shard_map/slice | solution.py:17
  342.6 1.6 scatter_custom_fusion.1
  345.7 2.0 collective-permute-start.8
  347.6 1.8 collective-permute-start.10
  351.5 1.7 multiply_add_fusion.5
  356.4 5.3 collective-permute-start.15
  361.7 3.9 collective-permute-start.14
  368.2 1.8 multiply_reduce_fusion.11
  370.0 76.1 %psum.108 = f32[]{:T(128)} all-reduce(f32[]{:T(128)} %get-tuple-element.32), channel_id=1, replica_groups=mesh['row'=8,'col'=32] {'row','col'}, use_global_device_ids=true, to_apply=%region_13.15 | all-reduce | flops 1 | bytes 8 | tf_op jit(solution)/shard_map/psum | solution.py:131
  448.1 74.3 %psum.109 = f32[]{:T(128)} all-reduce(f32[]{:T(128)} %multiply_reduce_fusion.10), channel_id=1, replica_groups=mesh['row'=8,'col'=32] {'row','col'}, use_global_device_ids=true, to_apply=%region_15.17 | all-reduce | flops 1 | bytes 8 | tf_op jit(solution)/shard_map/psum | solution.py:131
  522.3 2.8 multiply_reduce_fusion.9
  525.1 73.4 %psum.110 = f32[]{:T(128)} all-reduce(f32[]{:T(128)} %get-tuple-element.30), channel_id=1, replica_groups=mesh['row'=8,'col'=32] {'row','col'}, use_global_device_ids=true, to_apply=%region_17.19 | all-reduce | flops 1 | bytes 8 | tf_op jit(solution)/shard_map/psum | solution.py:89
  599.2 7.8 fusion.8
  607.0 1.9 copy-done.2
  609.6 2.0 gather_fusion.6
  611.5 14.6 %slice_reduce_fusion.7 = (f32[32,256]{1,0:T(8,128)S(1)}, f32[32,256]{1,0:T(8,128)S(1)}, f32[32,256]{1,0:T(8,128)S(1)}, f32[32,256]{1,0:T(8,128)}) fusion(f32[4,32,256]{0,2,1:T(8,128)} %copy-done.2), kind=kLoop, calls=%fused_computation.54 | loop fusion | bytes 262144 | tf_op jit(solution)/shard_map/slice | solution.py:17
  634.3 1.6 scatter_custom_fusion.2
  637.3 1.6 collective-permute-start.16
  641.0 1.7 multiply_add_fusion.3
  642.7 1.8 collective-permute-start.18
  649.4 6.9 collective-permute-start.23
  661.0 1.8 multiply_reduce_fusion.8
  662.8 76.5 %psum.111 = f32[]{:T(128)} all-reduce(f32[]{:T(128)} %get-tuple-element.28), channel_id=1, replica_groups=mesh['row'=8,'col'=32] {'row','col'}, use_global_device_ids=true, to_apply=%region_22.24 | all-reduce | flops 1 | bytes 8 | tf_op jit(solution)/shard_map/psum | solution.py:131
  741.7 73.6 %psum.112 = f32[]{:T(128)} all-reduce(f32[]{:T(128)} %multiply_reduce_fusion.7), channel_id=1, replica_groups=mesh['row'=8,'col'=32] {'row','col'}, use_global_device_ids=true, to_apply=%region_24.26 | all-reduce | flops 1 | bytes 8 | tf_op jit(solution)/shard_map/psum | solution.py:131
  816.7 2.8 multiply_reduce_fusion.6
  819.4 74.1 %psum.113 = f32[]{:T(128)} all-reduce(f32[]{:T(128)} %get-tuple-element.26), channel_id=1, replica_groups=mesh['row'=8,'col'=32] {'row','col'}, use_global_device_ids=true, to_apply=%region_26.28 | all-reduce | flops 1 | bytes 8 | tf_op jit(solution)/shard_map/psum | solution.py:131
  894.8 73.5 %psum.114 = f32[]{:T(128)} all-reduce(f32[]{:T(128)} %multiply_reduce_fusion.5), channel_id=1, replica_groups=mesh['row'=8,'col'=32] {'row','col'}, use_global_device_ids=true, to_apply=%region_28.30 | all-reduce | flops 1 | bytes 8 | tf_op jit(solution)/shard_map/psum | solution.py:89
  970.5 9.1 fusion.11
  979.6 2.0 gather_fusion.7
  983.1 14.6 %slice_reduce_fusion.3 = (f32[32,256]{1,0:T(8,128)S(1)}, f32[32,256]{1,0:T(8,128)S(1)}, f32[32,256]{1,0:T(8,128)S(1)}, f32[32,256]{1,0:T(8,128)}) fusion(f32[4,32,256]{0,2,1:T(8,128)} %fusion.11), kind=kLoop, calls=%fused_computation.50 | loop fusion | bytes 262144 | tf_op jit(solution)/shard_map/slice | solution.py:17
  1005.2 1.6 scatter_custom_fusion.3
  1008.2 2.0 collective-permute-start.24
  1011.4 1.8 multiply_add_fusion.1
  1014.1 1.8 collective-permute-start.26
  1017.2 2.0 collective-permute-done.25
  1020.6 6.8 collective-permute-start.31
  1032.0 1.8 multiply_reduce_fusion.4
  1033.7 76.6 %psum.115 = f32[]{:T(128)} all-reduce(f32[]{:T(128)} %get-tuple-element.24), channel_id=1, replica_groups=mesh['row'=8,'col'=32] {'row','col'}, use_global_device_ids=true, to_apply=%region_33.35 | all-reduce | flops 1 | bytes 8 | tf_op jit(solution)/shard_map/psum | solution.py:131
  1112.9 73.5 %psum.116 = f32[]{:T(128)} all-reduce(f32[]{:T(128)} %multiply_reduce_fusion.3), channel_id=1, replica_groups=mesh['row'=8,'col'=32] {'row','col'}, use_global_device_ids=true, to_apply=%region_35.37 | all-reduce | flops 1 | bytes 8 | tf_op jit(solution)/shard_map/psum | solution.py:131
  1187.6 1.9 multiply_reduce_fusion.2
  1189.5 74.2 %psum.117 = f32[]{:T(128)} all-reduce(f32[]{:T(128)} %get-tuple-element.22), channel_id=1, replica_groups=mesh['row'=8,'col'=32] {'row','col'}, use_global_device_ids=true, to_apply=%region_37.39 | all-reduce | flops 1 | bytes 8 | tf_op jit(solution)/shard_map/psum | solution.py:131
  1266.3 73.4 %psum.118 = f32[]{:T(128)} all-reduce(f32[]{:T(128)} %multiply_reduce_fusion.1), channel_id=1, replica_groups=mesh['row'=8,'col'=32] {'row','col'}, use_global_device_ids=true, to_apply=%region_39.41 | all-reduce | flops 1 | bytes 8 | tf_op jit(solution)/shard_map/psum | solution.py:131
  1339.7 1.9 multiply_reduce_fusion
  1342.8 74.3 %psum.119 = f32[]{:T(128)} all-reduce(f32[]{:T(128)} %multiply_reduce_fusion), channel_id=1, replica_groups=mesh['row'=8,'col'=32] {'row','col'}, use_global_device_ids=true, to_apply=%region_41.43 | all-reduce | flops 1 | bytes 8 | tf_op jit(solution)/shard_map/psum | solution.py:89
  1418.1 9.1 fusion.14
  1427.2 3.5 copy.158
  (219 shorter events, 88.1 us)
Async XLA Ops:
  0.7 105.6 %copy-start.15 = (pred[32]{0:T(512)(128)(4,1)}, pred[32]{0:T(512)(128)(4,1)S(1)}, u32[]{:S(2)}) copy-start(pred[32]{0:T(512)(128)(4,1)S(1)} %and_bitcast_fusion) | copy-start | bytes 100
  4.4 102.1 %copy-start.18 = (s32[64]{0:T(128)}, s32[64]{0:T(128)S(1)}, u32[]{:S(2)}) copy-start(s32[64]{0:T(128)S(1)} %fusion.75) | copy-start | bytes 772
  95.0 11.3 copy-start.14
  95.0 16.0 %copy-start.17 = (s32[32]{0:T(128)S(1)}, s32[32]{0:T(128)}, u32[]{:S(2)}) copy-start(s32[32]{0:T(128)} %param.19) | copy-start | bytes 388
  102.8 1.9 copy-start
  107.3 3.6 copy-start.12
  108.0 22.5 %collective-permute-start = (f32[4,32]{0,1:T(8,128)}, f32[4,32]{0,1:T(8,128)}, u32[]{:S(2)}, u32[]{:S(2)}) collective-permute-start(f32[4,32]{0,1:T(8,128)} %get-tuple-element.82), channel_id=1, source_target_pairs={{0,30},{1,31},{2,0},{3,1},{4,2},{5,3},{6,4},{7,5},{8,6},{9,7},{10,... | collective-permute-start | bytes 1544 | tf_op jit(solution)/shard_map/ppermute | solution.py:13
  109.2 21.4 %collective-permute-start.3 = (f32[4,32]{0,1:T(8,128)}, f32[4,32]{0,1:T(8,128)}, u32[]{:S(2)}, u32[]{:S(2)}) collective-permute-start(f32[4,32]{0,1:T(8,128)} %get-tuple-element.83), channel_id=1, source_target_pairs={{0,2},{1,3},{2,4},{3,5},{4,6},{5,7},{6,8},{7,9},{8,10},{9,11},{10,... | collective-permute-start | bytes 1544 | tf_op jit(solution)/shard_map/ppermute | solution.py:13
  109.5 21.1 %collective-permute-start.2 = (f32[4,32]{0,1:T(8,128)}, f32[4,32]{0,1:T(8,128)}, u32[]{:S(2)}, u32[]{:S(2)}) collective-permute-start(f32[4,32]{0,1:T(8,128)} %get-tuple-element.84), channel_id=1, source_target_pairs={{0,1},{1,2},{2,3},{3,4},{4,5},{5,6},{6,7},{7,8},{8,9},{9,10},{10,1... | collective-permute-start | bytes 1544 | tf_op jit(solution)/shard_map/ppermute | solution.py:13
  110.6 20.0 %collective-permute-start.1 = (f32[4,32]{0,1:T(8,128)}, f32[4,32]{0,1:T(8,128)}, u32[]{:S(2)}, u32[]{:S(2)}) collective-permute-start(f32[4,32]{0,1:T(8,128)} %get-tuple-element.85), channel_id=1, source_target_pairs={{0,31},{1,0},{2,1},{3,2},{4,3},{5,4},{6,5},{7,6},{8,7},{9,8},{10,9... | collective-permute-start | bytes 1544 | tf_op jit(solution)/shard_map/ppermute | solution.py:13
  111.0 15.3 %copy-start.13 = (bf16[4,4,32,256]{3,2,1,0:T(8,128)(2,1)S(1)}, bf16[4,4,32,256]{3,2,1,0:T(8,128)(2,1)}, u32[]{:S(2)}) copy-start(bf16[4,4,32,256]{3,2,1,0:T(8,128)(2,1)} %param.13) | copy-start | bytes 786436
  111.0 39.6 %copy-start.3 = (f32[4,32,256]{2,1,0:T(8,128)S(1)}, f32[4,32,256]{2,1,0:T(8,128)}, u32[]{:S(2)}) copy-start(f32[4,32,256]{2,1,0:T(8,128)} %param.11) | copy-start | bytes 393220
  125.6 24.9 %copy-start.4 = (bf16[4,4,32,256]{3,2,1,0:T(8,128)(2,1)S(1)}, bf16[4,4,32,256]{3,2,1,0:T(8,128)(2,1)}, u32[]{:S(2)}) copy-start(bf16[4,4,32,256]{3,2,1,0:T(8,128)(2,1)} %param.12) | copy-start | bytes 786436
  127.3 1.9 copy-start.8
  127.3 177.9 %copy-start.7 = (f32[4,32,256]{2,1,0:T(8,128)}, f32[4,32,256]{2,1,0:T(8,128)S(1)}, u32[]{:S(2)}) copy-start(f32[4,32,256]{2,1,0:T(8,128)S(1)} %get-tuple-element.44) | copy-start | bytes 393220
  127.4 224.1 %copy-start.6 = (f32[4,32,256]{2,1,0:T(8,128)}, f32[4,32,256]{2,1,0:T(8,128)S(1)}, u32[]{:S(2)}) copy-start(f32[4,32,256]{2,1,0:T(8,128)S(1)} %get-tuple-element.43) | copy-start | bytes 393220
  127.4 513.6 %copy-start.5 = (f32[4,32,256]{2,1,0:T(8,128)}, f32[4,32,256]{2,1,0:T(8,128)S(1)}, u32[]{:S(2)}) copy-start(f32[4,32,256]{2,1,0:T(8,128)S(1)} %get-tuple-element.42) | copy-start | bytes 393220
  131.4 11.4 collective-permute-start.4
  132.5 13.3 collective-permute-start.7
  136.8 8.3 collective-permute-start.6
  142.7 1.2 collective-permute-start.5
  315.3 1.9 copy-start.1
  345.7 8.7 collective-permute-start.8
  347.6 6.7 collective-permute-start.11
  347.6 6.7 collective-permute-start.10
  349.5 4.9 collective-permute-start.9
  355.2 10.4 collective-permute-start.12
  356.4 10.4 collective-permute-start.15
  361.7 5.1 collective-permute-start.14
  365.6 1.2 collective-permute-start.13
  370.0 78.0 %copy-start.9 = (f32[4,32,256]{2,1,0:T(8,128)}, f32[4,32,256]{2,1,0:T(8,128)S(1)}, u32[]{:S(2)}) copy-start(f32[4,32,256]{2,1,0:T(8,128)S(1)} %get-tuple-element.33) | copy-start | bytes 393220
  607.0 1.9 copy-start.2
  637.3 9.3 collective-permute-start.16
  639.0 7.7 collective-permute-start.19
  642.7 3.9 collective-permute-start.18
  644.5 3.6 collective-permute-start.17
  648.9 9.3 collective-permute-start.20
  649.4 10.1 collective-permute-start.23
  656.4 3.2 collective-permute-start.22
  657.4 1.6 collective-permute-start.21
  662.8 153.2 %copy-start.11 = (f32[4,32,256]{2,1,0:T(8,128)}, f32[4,32,256]{2,1,0:T(8,128)S(1)}, u32[]{:S(2)}) copy-start(f32[4,32,256]{2,1,0:T(8,128)S(1)} %get-tuple-element.29) | copy-start | bytes 393220
  819.4 148.9 %copy-start.10 = (f32[4,32,256]{2,1,0:T(8,128)}, f32[4,32,256]{2,1,0:T(8,128)S(1)}, u32[]{:S(2)}) copy-start(f32[4,32,256]{2,1,0:T(8,128)S(1)} %get-tuple-element.27) | copy-start | bytes 393220
  983.1 16.0 %copy-start.16 = (pred[32]{0:T(512)(128)(4,1)S(1)}, pred[32]{0:T(512)(128)(4,1)}, u32[]{:S(2)}) copy-start(pred[32]{0:T(512)(128)(4,1)} %copy-done.15) | copy-start | bytes 100
  1008.2 8.9 collective-permute-start.24
  1010.3 6.9 collective-permute-start.27
  1014.1 3.1 collective-permute-start.26
  1015.9 3.4 collective-permute-start.25
  1020.0 9.1 collective-permute-start.28
  1020.6 9.9 collective-permute-start.31
  1027.3 3.2 collective-permute-start.30
  1028.0 1.9 collective-permute-start.29
where the time goes:
time: 1450 us; the launch traced here: 1430 us
  blocking collectives  1130 us (78%)
  local copies, waits for them, and re-layouts  121 us (8%)
  other arithmetic  106 us (7%)
  starting transfers between devices  52.8 us (4%)
  between operations  18 us (1%)
    psum x10, blocking collectives, body(): product = lax.psum(jnp.sum(basis[i] * work), ('row', 'col'))  748 us
    psum x5, blocking collectives, global_sum(): return lax.psum(value, ('row', 'col'))  377 us
    slice x4, local copies, waits for them, and re-layouts, block_transpose(): out = blocks[0].astype(jnp.float32) * vec[0]  58.5 us
    ppermute x32, starting transfers between devices, from_behind(): return lax.ppermute(value, axis, pairs)  52.8 us
    add x5, other arithmetic, block_apply(): out = out + blocks[:, index].astype(jnp.float32) * vec[index]  41.6 us
  transfers between devices with their start and end apart: 32, of which 8 were waited for; matrix products, arithmetic and copies ran while one was open for 2% of the time, Pallas kernels for 0%

commit v1 on v0

v1 whole, which is shorter than its diff:
```python
import functools

import jax
import jax.numpy as jnp
from jax import lax
from jax.experimental import pallas as pl
from jax.experimental.pallas import tpu as pltpu
from jax.sharding import PartitionSpec as P

ITERS = 4
REACH = 2
SPAN = 2 * REACH
PIECES = 2 * SPAN + 1
SHIFT = 1.0
CHUNK = 16
MESH = pl.DeviceIdType.MESH
F32 = jnp.float32
BF16 = jnp.bfloat16


def iota(shape, dim):
    return lax.broadcasted_iota(jnp.int32, shape, dim)


def split3(value):
    high = value.astype(BF16)
    rest = value - high.astype(F32)
    middle = rest.astype(BF16)
    low = (rest - middle.astype(F32)).astype(BF16)
    return high, middle, low


def dot(a, b):
    return lax.dot_general(a, b, (((1,), (0,)), ((), ())), preferred_element_type=F32)


def end_row(first, last):
    empty = jnp.zeros_like(first)
    return jnp.concatenate([first, empty, last, empty], axis=1)


def least_squares(hess, beta, steps):
    upper = [list(line) for line in hess]
    target = [beta] + [None] * steps
    cosines = []
    sines = []
    for k in range(steps):
        for i in range(k):
            temp = cosines[i] * upper[i][k] + sines[i] * upper[i + 1][k]
            upper[i + 1][k] = -sines[i] * upper[i][k] + cosines[i] * upper[i + 1][k]
            upper[i][k] = temp
        inverse = 1.0 / jnp.sqrt(upper[k][k] * upper[k][k] + upper[k + 1][k] * upper[k + 1][k])
        cosines.append(upper[k][k] * inverse)
        sines.append(upper[k + 1][k] * inverse)
        upper[k][k] = cosines[k] * upper[k][k] + sines[k] * upper[k + 1][k]
        target[k + 1] = -sines[k] * target[k]
        target[k] = cosines[k] * target[k]
    coeffs = [None] * steps
    for k in range(steps - 1, -1, -1):
        total = target[k]
        for j in range(k + 1, steps):
            total = total - upper[k][j] * coeffs[j]
        coeffs[k] = total / upper[k][k]
    return coeffs


def krylov_coeffs(gram):
    size = ITERS + 1
    low = [[None] * size for _ in range(size)]
    for j in range(size):
        total = gram[j, j]
        for k in range(j):
            total = total - low[j][k] * low[j][k]
        total = jnp.maximum(total, 1e-7 * gram[j, j])
        inverse = lax.rsqrt(total)
        low[j][j] = total * inverse
        for i in range(j + 1, size):
            total = gram[j, i]
            for k in range(j):
                total = total - low[i][k] * low[j][k]
            low[i][j] = total * inverse
    hess = [[None] * ITERS for _ in range(size)]
    for k in range(ITERS):
        for i in range(k + 2):
            hess[i][k] = low[k + 1][i]
            if i <= k:
                hess[i][k] = hess[i][k] + SHIFT * low[k][i]
    return least_squares(hess, low[0][0], ITERS)


PAIRS = [(i, j) for j in range(ITERS + 1) for i in range(j + 1)]
GRAM_ROWS = 16


def kernel(
    rows,
    columns,
    right_hbm,
    diag_hbm,
    lower_hbm,
    upper_hbm,
    precond_hbm,
    out_hbm_blocks,
    in_hbm_blocks,
    junction_hbm,
    length_hbm,
    result_hbm,
    right,
    diag,
    lower,
    upper,
    precond,
    jout,
    jin,
    junction,
    length,
    basis,
    image,
    bulk,
    result,
    sends,
    recvs,
    gram_own,
    gram_one,
    gram_two,
    in_sems,
    out_sems,
    near_send,
    near_recv,
    one_send,
    one_recv,
    two_send,
    two_recv,
):
    row = lax.axis_index("row")
    col = lax.axis_index("col")
    count_one = 2 * rows
    count_two = columns // 2
    core = col % 2
    place = col // 2
    mine_one = row * 2 + core
    mine_two = place

    def near(offset):
        return (row, (col + offset + columns) % columns)

    def member_one(step):
        index = (mine_one + step) % count_one
        return (index // 2, place * 2 + index % 2)

    def member_two(step):
        index = (mine_two + step) % count_two
        return (row, index * 2 + core)

    loads = [
        pltpu.make_async_copy(source, target, in_sems.at[index])
        for index, (source, target) in enumerate(
            [
                (length_hbm, length),
                (junction_hbm, junction),
                (out_hbm_blocks, jout),
                (in_hbm_blocks, jin),
                (right_hbm, right),
                (precond_hbm, precond),
                (diag_hbm, diag),
                (lower_hbm, lower),
                (upper_hbm, upper),
            ]
        )
    ]
    for load in loads:
        load.start()

    barrier = pltpu.get_barrier_semaphore()
    partners = [near(offset) for offset in (-3, -1, 1, 3)]
    partners += [member_one(step) for step in range(1, count_one)]
    partners += [member_two(step) for step in range(1, count_two)]
    for partner in partners:
        pl.semaphore_signal(barrier, inc=1, device_id=partner, device_id_type=MESH)

    sends[...] = jnp.zeros_like(sends)
    for load in loads[:6]:
        load.wait()

    lane = iota((1, 128), 1)
    lengths = length[...]
    length_row = end_row(lengths, lengths)
    slot_row = jnp.where(
        (lane & 32) != 0, -1, end_row(jnp.zeros_like(lengths), lengths - 1)
    )
    extract = (iota((256, 128), 0) == slot_row).astype(F32).astype(BF16)
    ids = junction[...] + 1
    id_row = jnp.where((lane & 32) != 0, -1, end_row(ids[0:1], ids[1:2]))
    square = iota((128, 128), 0) == iota((128, 128), 1)
    slot_col = jnp.sum(jnp.where(square, slot_row.astype(F32), 0.0), axis=1, keepdims=True)
    id_col = jnp.sum(jnp.where(square, id_row.astype(F32), 0.0), axis=1, keepdims=True)
    insert = (iota((128, 256), 1).astype(F32) == slot_col).astype(F32)
    insert = jnp.concatenate([insert] * 3, axis=0).astype(BF16)
    length_col = jnp.sum(
        jnp.where(square[:32], length_row.astype(F32), 0.0), axis=1, keepdims=True
    )
    active = iota((32, 256), 1).astype(F32) < length_col
    single = ((length_row == 1) & ((lane & 32) == 0)).astype(F32)
    own_pipe = (iota((32, 128), 0) == (iota((32, 128), 1) & 63))[None]

    def ends_of(value):
        total = sum(dot(part, extract) for part in split3(value.reshape(128, 256)))
        return jnp.sum(jnp.where(own_pipe, total.reshape(4, 32, 128), 0.0), axis=1)

    def at_ends(value):
        spread = jnp.where(own_pipe, value[:, None, :], 0.0).reshape(128, 128)
        return dot(jnp.concatenate(split3(spread), axis=1), insert).reshape(4, 32, 256)

    def block_row(ref, a):
        return end_row(ref[0, a], ref[1, a])

    def apply(blocks, value):
        total = blocks[0] * value[0:1]
        for a in range(1, 4):
            total = total + blocks[a] * value[a : a + 1]
        return total

    out_blocks = [block_row(jout, a) for a in range(4)]
    in_blocks = [block_row(jin, a) for a in range(4)]
    pre_ends = dot(precond[...].reshape(512, 256), extract).reshape(16, 32, 128)
    pre_ends = jnp.sum(jnp.where(own_pipe, pre_ends, 0.0), axis=1)
    to_balance = [
        sum(out_blocks[a] * pre_ends[a * 4 + b : a * 4 + b + 1] for a in range(4)) for b in range(4)
    ]

    start = jnp.where(active[None], right[...], 0.0)
    basis[0] = start
    end_values = [ends_of(start)]

    def post(step, balance):
        sends[step, 0, 0:4] = balance
        sends[step, 1, 0:4] = pltpu.roll(balance, 32, 1)
        copies = []
        for index, offset in enumerate(o for o in range(-SPAN, SPAN + 1) if o != 0):
            copy = pltpu.make_async_remote_copy(
                src_ref=sends.at[step, offset % 2],
                dst_ref=recvs.at[step, SPAN - offset],
                send_sem=near_send.at[step, index],
                recv_sem=near_recv.at[step, index],
                device_id=near(offset),
                device_id_type=MESH,
            )
            copy.start()
            copies.append(copy)
        recvs[step, SPAN] = sends[step, 0]
        return copies

    def advance(step):
        if step == 0:
            for load in loads[6:]:
                load.wait()
        for first in range(0, 32, CHUNK):
            part = slice(first, first + CHUNK)
            vec = [basis[step, b, part] for b in range(4)]
            x = []
            for a in range(4):
                total = precond[a, 0, part].astype(F32) * vec[0]
                for b in range(1, 4):
                    total = total + precond[a, b, part].astype(F32) * vec[b]
                image[step, a, part] = total
                x.append(total)
            keep = active[part]
            slot = iota((CHUNK, 256), 1)
            for b in range(4):
                sums = []
                for blocks in (diag, lower, upper):
                    total = blocks[0, b, part].astype(F32) * x[0]
                    for a in range(1, 4):
                        total = total + blocks[a, b, part].astype(F32) * x[a]
                    sums.append(total)
                following = jnp.where(slot == 255, 0.0, pltpu.roll(sums[1], 255, 1))
                preceding = jnp.where(slot == 0, 0.0, pltpu.roll(sums[2], 1, 1))
                total = jnp.where(keep, sums[0] + following + preceding, 0.0)
                bulk[b, part] = total - SHIFT * vec[b]

    def inner(left, right_part):
        total = jnp.sum(left * right_part, axis=(0, 1)).reshape(1, 256)
        return total[:, :128] + total[:, 128:]

    balance = apply(to_balance, end_values[0])
    sends[0, 0, 4:5] = jnp.maximum(id_row, 0).astype(F32)
    sends[0, 1, 4:5] = pltpu.roll(jnp.maximum(id_row, 0).astype(F32), 32, 1)
    pl.semaphore_wait(barrier, len(partners))

    pending = []
    matches = None
    for step in range(ITERS):
        copies = post(step, balance)
        pending += copies
        advance(step)
        bulk_ends = ends_of(bulk[...])
        if step == ITERS - 1:
            for index, (i, j) in enumerate(PAIRS):
                other = bulk[...] if j == ITERS else basis[j]
                value = bulk[...] if i == ITERS else basis[i]
                gram_own[0, index : index + 1] = inner(value, other)
            gram_own[0, len(PAIRS) : GRAM_ROWS] = jnp.zeros((GRAM_ROWS - len(PAIRS), 128), F32)
        for copy in copies:
            copy.wait_recv()
        joined = jnp.concatenate(
            [
                recvs[step, index] + recvs[step, index + 1]
                if index + 1 < PIECES
                else recvs[step, index]
                for index in range(0, PIECES, 2)
            ],
            axis=1,
        )
        if step == 0:
            matches = (id_col == joined[4:5]).astype(F32).T.astype(BF16)
        high = joined.astype(BF16).astype(F32)
        middle = (joined - high).astype(BF16).astype(F32)
        left = jnp.concatenate([high, middle, joined - high - middle, jnp.zeros_like(high)], axis=0)
        sums = dot(left.astype(BF16), matches)
        sums = sums[0:4] + sums[8:12] + sums[16:20]
        added = apply(in_blocks, sums)
        both = added + single * pltpu.roll(added, 64, 1)
        if step < ITERS - 1:
            end_values.append(bulk_ends + both)
            balance = apply(to_balance, end_values[-1])
            basis[step + 1] = bulk[...] + at_ends(added)
        else:
            for index, (i, j) in enumerate(PAIRS):
                if j == ITERS:
                    weight = 2.0 * bulk_ends + both if i == ITERS else end_values[i]
                    row_sum = jnp.sum(weight * added, axis=0, keepdims=True)
                    gram_own[0, index : index + 1] = gram_own[0, index : index + 1] + row_sum

    def all_sum(own, box, mine, member, count, send, recv):
        copies = []
        for step in range(1, count):
            copy = pltpu.make_async_remote_copy(
                src_ref=own,
                dst_ref=box.at[mine],
                send_sem=send.at[step],
                recv_sem=recv.at[step],
                device_id=member(step),
                device_id_type=MESH,
            )
            copy.start()
            copies.append(copy)
        box[mine] = own[...]
        for copy in copies:
            copy.wait_recv()
        return copies, jnp.sum(box[...], axis=0)

    copies, total = all_sum(
        gram_own.at[0], gram_one, mine_one, member_one, count_one, one_send, one_recv
    )
    pending += copies
    gram_own[1] = total
    copies, total = all_sum(
        gram_own.at[1], gram_two, mine_two, member_two, count_two, two_send, two_recv
    )
    pending += copies
    total = jnp.sum(total, axis=1, keepdims=True)
    gram = {pair: total[index : index + 1] for index, pair in enumerate(PAIRS)}
    coeffs = krylov_coeffs(gram)
    stores = []
    for a in range(4):
        value = coeffs[0] * image[0, a]
        for k in range(1, ITERS):
            value = value + coeffs[k] * image[k, a]
        result[a] = value
        store = pltpu.make_async_copy(result.at[a], result_hbm.at[a], out_sems.at[a])
        store.start()
        stores.append(store)
    for store in stores:
        store.wait()
    for copy in pending:
        copy.wait_send()


def body(rows, columns, right_side, diag, lower, upper, precond, jout, jin, junction, length):
    pipes, slots = right_side.shape[1:]
    length = length.reshape(1, pipes)
    operands = (right_side, diag, lower, upper, precond, jout, jin, junction, length)
    inputs = [pltpu.VMEM(value.shape, value.dtype) for value in operands]
    count_one, count_two = 2 * rows, columns // 2
    near_count = PIECES - 1
    return pl.pallas_call(
        functools.partial(kernel, rows, columns),
        out_shape=jax.ShapeDtypeStruct(right_side.shape, F32),
        in_specs=[pl.BlockSpec(memory_space=pl.ANY)] * len(operands),
        out_specs=pl.BlockSpec(memory_space=pl.ANY),
        scratch_shapes=inputs
        + [
            pltpu.VMEM((ITERS, 4, pipes, slots), F32),
            pltpu.VMEM((ITERS, 4, pipes, slots), F32),
            pltpu.VMEM((4, pipes, slots), F32),
            pltpu.VMEM((4, pipes, slots), F32),
            pltpu.VMEM((ITERS, 2, 8, 128), F32),
            pltpu.VMEM((ITERS, PIECES, 8, 128), F32),
            pltpu.VMEM((2, GRAM_ROWS, 128), F32),
            pltpu.VMEM((count_one, GRAM_ROWS, 128), F32),
            pltpu.VMEM((count_two, GRAM_ROWS, 128), F32),
            pltpu.SemaphoreType.DMA((len(operands),)),
            pltpu.SemaphoreType.DMA((4,)),
            pltpu.SemaphoreType.DMA((ITERS, near_count)),
            pltpu.SemaphoreType.DMA((ITERS, near_count)),
            pltpu.SemaphoreType.DMA((count_one,)),
            pltpu.SemaphoreType.DMA((count_one,)),
            pltpu.SemaphoreType.DMA((count_two,)),
            pltpu.SemaphoreType.DMA((count_two,)),
        ],
        compiler_params=pltpu.CompilerParams(
            collective_id=0, has_side_effects=True, vmem_limit_bytes=32 * 1024 * 1024
        ),
    )(*operands)


def solution(mesh):
    in_specs = (
        P(None, ("row", "col"), None),
        P(None, None, ("row", "col"), None),
        P(None, None, ("row", "col"), None),
        P(None, None, ("row", "col"), None),
        P(None, None, ("row", "col"), None),
        P(None, None, None, ("row", "col")),
        P(None, None, None, ("row", "col")),
        P(None, ("row", "col")),
        P(("row", "col")),
    )
    out_specs = P(None, ("row", "col"), None)
    run = functools.partial(body, mesh.shape["row"], mesh.shape["col"])
    return jax.shard_map(run, mesh=mesh, in_specs=in_specs, out_specs=out_specs, check_vma=False)
```

time: 1450 us -> 49 us (0.03); the launches traced: 1430 us -> 48.6 us
  blocking collectives: 1130 us -> 0 us
  local copies, waits for them, and re-layouts: 121 us -> 7.49 us
  other arithmetic: 106 us -> 0 us
  starting transfers between devices: 52.8 us -> 0 us
  Pallas kernels: 0 us -> 41.1 us
  between operations: 18 us -> 0.02 us
    psum x15 -> x0, blocking collectives: 1130 us -> none  [the longest x10 748 us: body(): product = lax.psum(jnp.sum(basis[i] * work), ('row', 'col'))]
    slice x35 -> x0, local copies, waits for them, and re-layouts: 82.3 us -> none  [the longest x4 58.5 us: block_transpose(): out = blocks[0].astype(jnp.float32) * vec[0]]
    add x18 -> x0, other arithmetic: 54 us -> none  [the longest x5 41.6 us: block_apply(): out = out + blocks[:, index].astype(jnp.float32) * vec[index]]
    ppermute x32 -> x0, starting transfers between devices: 52.8 us -> none  [from_behind(): return lax.ppermute(value, axis, pairs)]
    pallas_call x0 -> x1, Pallas kernels: none -> 41.1 us  [body(): pl.pallas_call(functools.partial(kernel, rows, columns), out_shape=jax.Sh...]
    reduce_sum x23 -> x0, other arithmetic: 32.3 us -> none  [the longest x10 17.5 us: body(): product = lax.psum(jnp.sum(basis[i] * work), ('row', 'col'))]
    gather x12 -> x0, local copies, waits for them, and re-layouts: 15.3 us -> none  [the longest x8 11.4 us: body(): last = jnp.take_along_axis(vec, last_slot[None, :, None], axis=2)[:, :, 0]]
  transfers between devices with their start and end apart: 32 -> 0, of which waited for: 8 -> 0; matrix products, arithmetic and copies ran while one was open for 2% -> 0% of each run, Pallas kernels for 0% -> 0%
where the time goes in v1:
time: 49 us; the launch traced here: 48.6 us
  Pallas kernels  41.1 us (84%)
  local copies, waits for them, and re-layouts  7.49 us (15%)
    pallas_call x1, Pallas kernels, body(): pl.pallas_call(functools.partial(kernel, rows, columns), out_shape=jax.Sh...  41.1 us
    unnamed x19, local copies, waits for them, and re-layouts  7.49 us

profile of v1, /device:TPU:1, one launch (start us, length us, event | category | flops | bytes accessed | tf_op | source)
XLA Modules:
  0.0 48.6 jit_solution(11260139087812822424)
XLA Ops:
  0.0 0.0 copy-start.8
  0.0 0.0 copy-start.7
  0.0 0.7 %copy-done.8 = s32[32]{0:T(128)S(1)} copy-done((s32[32]{0:T(128)S(1)}, s32[32]{0:T(128)}, u32[]{:S(2)}) %copy-start.8) | copy-done | bytes 152
  0.7 0.0 copy-done.7
  0.7 0.0 copy-start
  0.7 0.9 %copy-done = bf16[4,4,32,256]{3,2,1,0:T(8,128)(2,1)S(1)} copy-done((bf16[4,4,32,256]{3,2,1,0:T(8,128)(2,1)S(1)}, bf16[4,4,32,256]{3,2,1,0:T(8,128)(2,1)}, u32[]{:S(2)}) %copy-start) | copy-done | bytes 262168
  1.6 0.0 copy-start.1
  1.6 0.9 %copy-done.1 = bf16[4,4,32,256]{3,2,1,0:T(8,128)(2,1)S(1)} copy-done((bf16[4,4,32,256]{3,2,1,0:T(8,128)(2,1)S(1)}, bf16[4,4,32,256]{3,2,1,0:T(8,128)(2,1)}, u32[]{:S(2)}) %copy-start.1) | copy-done | bytes 262168
  2.6 0.0 copy-start.2
  2.6 0.9 %copy-done.2 = bf16[4,4,32,256]{3,2,1,0:T(8,128)(2,1)S(1)} copy-done((bf16[4,4,32,256]{3,2,1,0:T(8,128)(2,1)S(1)}, bf16[4,4,32,256]{3,2,1,0:T(8,128)(2,1)}, u32[]{:S(2)}) %copy-start.2) | copy-done | bytes 262168
  3.5 0.0 copy-start.3
  3.5 0.9 %copy-done.3 = bf16[4,4,32,256]{3,2,1,0:T(8,128)(2,1)S(1)} copy-done((bf16[4,4,32,256]{3,2,1,0:T(8,128)(2,1)S(1)}, bf16[4,4,32,256]{3,2,1,0:T(8,128)(2,1)}, u32[]{:S(2)}) %copy-start.3) | copy-done | bytes 262168
  4.5 0.0 copy-start.4
  4.5 0.9 %copy-done.4 = f32[4,32,256]{2,1,0:T(8,128)S(1)} copy-done((f32[4,32,256]{2,1,0:T(8,128)S(1)}, f32[4,32,256]{2,1,0:T(8,128)}, u32[]{:S(2)}) %copy-start.4) | copy-done | bytes 131096
  5.4 0.0 copy-start.5
  5.4 0.7 %copy-done.5 = f32[2,4,4,32]{3,2,1,0:T(4,128)S(1)} copy-done((f32[2,4,4,32]{3,2,1,0:T(4,128)S(1)}, f32[2,4,4,32]{3,2,1,0:T(4,128)}, u32[]{:S(2)}) %copy-start.5) | copy-done | bytes 4120
  6.1 0.0 copy-start.6
  6.1 0.7 %copy-done.6 = f32[2,4,4,32]{3,2,1,0:T(4,128)S(1)} copy-done((f32[2,4,4,32]{3,2,1,0:T(4,128)S(1)}, f32[2,4,4,32]{3,2,1,0:T(4,128)}, u32[]{:S(2)}) %copy-start.6) | copy-done | bytes 4120
  6.8 41.1 %shard_map.91 = f32[4,32,256]{2,1,0:T(8,128)S(1)} custom-call(f32[4,32,256]{2,1,0:T(8,128)S(1)} %copy-done.4, bf16[4,4,32,256]{3,2,1,0:T(8,128)(2,1)S(1)} %copy-done, bf16[4,4,32,256]{3,2,1,0:T(8,128)(2,1)S(1)} %copy-done.1, bf16[4,4,32,256]{3,2,1,0:T(8,128)(2,1)S(1)} %copy-done.2, bf16[4,4,32,256]{3,2,1,0:T(8,128)(2,1)S(1)} %copy-done.3, ...), custom_call_target="tpu_custom_call" | custom-call | tf_op jit(solution)/shard_map/pallas_call | solution.py:386
  48.0 0.7 %copy.11 = f32[4,32,256]{2,1,0:T(8,128)} copy(f32[4,32,256]{2,1,0:T(8,128)S(1)} %shard_map.91) | data formatting | bytes 262144
Async XLA Ops:
  0.0 0.7 %copy-start.8 = (s32[32]{0:T(128)S(1)}, s32[32]{0:T(128)}, u32[]{:S(2)}) copy-start(s32[32]{0:T(128)} %param.17) | copy-start | bytes 388
  0.0 0.7 %copy-start.7 = (s32[2,32]{1,0:T(2,128)S(1)}, s32[2,32]{1,0:T(2,128)}, u32[]{:S(2)}) copy-start(s32[2,32]{1,0:T(2,128)} %junction_hbm.1) | copy-start | bytes 772
  0.7 0.9 %copy-start = (bf16[4,4,32,256]{3,2,1,0:T(8,128)(2,1)S(1)}, bf16[4,4,32,256]{3,2,1,0:T(8,128)(2,1)}, u32[]{:S(2)}) copy-start(bf16[4,4,32,256]{3,2,1,0:T(8,128)(2,1)} %diag_hbm.1) | copy-start | bytes 786436
  1.6 0.9 %copy-start.1 = (bf16[4,4,32,256]{3,2,1,0:T(8,128)(2,1)S(1)}, bf16[4,4,32,256]{3,2,1,0:T(8,128)(2,1)}, u32[]{:S(2)}) copy-start(bf16[4,4,32,256]{3,2,1,0:T(8,128)(2,1)} %lower_hbm.1) | copy-start | bytes 786436
  2.6 0.9 %copy-start.2 = (bf16[4,4,32,256]{3,2,1,0:T(8,128)(2,1)S(1)}, bf16[4,4,32,256]{3,2,1,0:T(8,128)(2,1)}, u32[]{:S(2)}) copy-start(bf16[4,4,32,256]{3,2,1,0:T(8,128)(2,1)} %upper_hbm.1) | copy-start | bytes 786436
  3.5 0.9 %copy-start.3 = (bf16[4,4,32,256]{3,2,1,0:T(8,128)(2,1)S(1)}, bf16[4,4,32,256]{3,2,1,0:T(8,128)(2,1)}, u32[]{:S(2)}) copy-start(bf16[4,4,32,256]{3,2,1,0:T(8,128)(2,1)} %precond_hbm.1) | copy-start | bytes 786436
  4.5 0.9 %copy-start.4 = (f32[4,32,256]{2,1,0:T(8,128)S(1)}, f32[4,32,256]{2,1,0:T(8,128)}, u32[]{:S(2)}) copy-start(f32[4,32,256]{2,1,0:T(8,128)} %right_hbm.1) | copy-start | bytes 393220
  5.4 0.7 %copy-start.5 = (f32[2,4,4,32]{3,2,1,0:T(4,128)S(1)}, f32[2,4,4,32]{3,2,1,0:T(4,128)}, u32[]{:S(2)}) copy-start(f32[2,4,4,32]{3,2,1,0:T(4,128)} %out_hbm_blocks.1) | copy-start | bytes 12292
  6.1 0.7 %copy-start.6 = (f32[2,4,4,32]{3,2,1,0:T(4,128)S(1)}, f32[2,4,4,32]{3,2,1,0:T(4,128)}, u32[]{:S(2)}) copy-start(f32[2,4,4,32]{3,2,1,0:T(4,128)} %in_hbm_blocks.1) | copy-start | bytes 12292

commit v2 on v1

--- a/solution.py
+++ b/solution.py
@@ -349,17 +349,19 @@
             copy.wait_recv()
         return copies, jnp.sum(box[...], axis=0)
 
+    partial = jnp.sum(gram_own[0], axis=1, keepdims=True)
+    eye = iota((GRAM_ROWS, 128), 0) == iota((GRAM_ROWS, 128), 1)
+    gram_own[1, 0:1] = jnp.sum(jnp.where(eye, partial, 0.0), axis=0, keepdims=True)
     copies, total = all_sum(
-        gram_own.at[0], gram_one, mine_one, member_one, count_one, one_send, one_recv
+        gram_own.at[1, 0:1], gram_one, mine_one, member_one, count_one, one_send, one_recv
     )
     pending += copies
-    gram_own[1] = total
+    gram_own[1, 8:9] = total
     copies, total = all_sum(
-        gram_own.at[1], gram_two, mine_two, member_two, count_two, two_send, two_recv
+        gram_own.at[1, 8:9], gram_two, mine_two, member_two, count_two, two_send, two_recv
     )
     pending += copies
-    total = jnp.sum(total, axis=1, keepdims=True)
-    gram = {pair: total[index : index + 1] for index, pair in enumerate(PAIRS)}
+    gram = {pair: total[:, index : index + 1] for index, pair in enumerate(PAIRS)}
     coeffs = krylov_coeffs(gram)
     stores = []
     for a in range(4):
@@ -397,8 +399,8 @@
             pltpu.VMEM((ITERS, 2, 8, 128), F32),
             pltpu.VMEM((ITERS, PIECES, 8, 128), F32),
             pltpu.VMEM((2, GRAM_ROWS, 128), F32),
-            pltpu.VMEM((count_one, GRAM_ROWS, 128), F32),
-            pltpu.VMEM((count_two, GRAM_ROWS, 128), F32),
+            pltpu.VMEM((count_one, 1, 128), F32),
+            pltpu.VMEM((count_two, 1, 128), F32),
             pltpu.SemaphoreType.DMA((len(operands),)),
             pltpu.SemaphoreType.DMA((4,)),
             pltpu.SemaphoreType.DMA((ITERS, near_count)),
@@ -409,7 +411,7 @@
             pltpu.SemaphoreType.DMA((count_two,)),
         ],
         compiler_params=pltpu.CompilerParams(
-            collective_id=0, has_side_effects=True, vmem_limit_bytes=32 * 1024 * 1024
+            collective_id=0, has_side_effects=True, vmem_limit_bytes=63 * 1024 * 1024
         ),
     )(*operands)
 

time: 49 us -> 42 us (0.86)
  local copies, waits for them, and re-layouts: 7.49 us -> 1.57 us
  Pallas kernels: 41.1 us -> 40.3 us
    unnamed x19 -> x1, local copies, waits for them, and re-layouts: 7.49 us -> 1.57 us
    pallas_call x1, Pallas kernels: 41.1 us -> 40.3 us  [body(): pl.pallas_call(functools.partial(kernel, rows, columns), out_shape=jax.Sh...]
where the time goes in v2:
time: 42 us; the launch traced here: 41.9 us
  Pallas kernels  40.3 us (96%)
  local copies, waits for them, and re-layouts  1.57 us (4%)
    pallas_call x1, Pallas kernels, body(): pl.pallas_call(functools.partial(kernel, rows, columns), out_shape=jax.Sh...  40.3 us
    unnamed x1, local copies, waits for them, and re-layouts  1.57 us

profile of v2, /device:TPU:1, one launch (start us, length us, event | category | flops | bytes accessed | tf_op | source)
XLA Modules:
  0.0 41.9 jit_solution(18176817997005588078)
XLA Ops:
  0.0 40.3 %shard_map.91 = f32[4,32,256]{2,1,0:T(8,128)} custom-call(f32[4,32,256]{2,1,0:T(8,128)} %right_hbm.1, bf16[4,4,32,256]{3,2,1,0:T(8,128)(2,1)} %diag_hbm.1, bf16[4,4,32,256]{3,2,1,0:T(8,128)(2,1)} %lower_hbm.1, bf16[4,4,32,256]{3,2,1,0:T(8,128)(2,1)} %upper_hbm.1, bf16[4,4,32,256]{3,2,1,0:T(8,128)(2,1)} %precond_hbm.1, f32[2,4,4,32]{3,2,1,0:T(4,128)} %out_hbm_blocks.1, ...), custom_call_target="tpu_custom_call" | custom-call | tf_op jit(solution)/shard_map/pallas_call | solution.py:388
  40.4 1.6 %copy.11 = f32[4,32,256]{2,1,0:T(8,128)} copy(f32[4,32,256]{2,1,0:T(8,128)} %shard_map.91) | data formatting | bytes 262144

commit v3 on v2

--- a/solution.py
+++ b/solution.py
@@ -10,7 +10,9 @@
 ITERS = 4
 REACH = 2
 SPAN = 2 * REACH
+FAR = 2 * SPAN
 PIECES = 2 * SPAN + 1
+PEERS = 2 * FAR + 1
 SHIFT = 1.0
 CHUNK = 16
 MESH = pl.DeviceIdType.MESH
@@ -104,7 +106,7 @@
     in_hbm_blocks,
     junction_hbm,
     length_hbm,
-    result_hbm,
+    result,
     right,
     diag,
     lower,
@@ -117,14 +119,14 @@
     basis,
     image,
     bulk,
-    result,
-    sends,
-    recvs,
+    sends_one,
+    sends_two,
+    recvs_one,
+    recvs_two,
     gram_own,
     gram_one,
     gram_two,
     in_sems,
-    out_sems,
     near_send,
     near_recv,
     one_send,
@@ -172,13 +174,14 @@
         load.start()
 
     barrier = pltpu.get_barrier_semaphore()
-    partners = [near(offset) for offset in (-3, -1, 1, 3)]
+    partners = [near(offset) for offset in range(1 - FAR, FAR, 2)]
     partners += [member_one(step) for step in range(1, count_one)]
     partners += [member_two(step) for step in range(1, count_two)]
     for partner in partners:
         pl.semaphore_signal(barrier, inc=1, device_id=partner, device_id_type=MESH)
 
-    sends[...] = jnp.zeros_like(sends)
+    sends_one[...] = jnp.zeros_like(sends_one)
+    sends_two[...] = jnp.zeros_like(sends_two)
     for load in loads[:6]:
         load.wait()
 
@@ -189,11 +192,15 @@
         (lane & 32) != 0, -1, end_row(jnp.zeros_like(lengths), lengths - 1)
     )
     extract = (iota((256, 128), 0) == slot_row).astype(F32).astype(BF16)
-    ids = junction[...] + 1
-    id_row = jnp.where((lane & 32) != 0, -1, end_row(ids[0:1], ids[1:2]))
+    ids = junction[...]
+    owned = ids % 32
+    ids = (ids // 32 - col + REACH + columns) % columns * 32 + owned
+    slot_of_junction_row = jnp.where((lane & 32) != 0, -1, end_row(ids[0:1], ids[1:2])).astype(F32)
     square = iota((128, 128), 0) == iota((128, 128), 1)
     slot_col = jnp.sum(jnp.where(square, slot_row.astype(F32), 0.0), axis=1, keepdims=True)
-    id_col = jnp.sum(jnp.where(square, id_row.astype(F32), 0.0), axis=1, keepdims=True)
+    slot_of_junction_col = jnp.sum(
+        jnp.where(square, slot_of_junction_row, 0.0), axis=1, keepdims=True
+    )
     insert = (iota((128, 256), 1).astype(F32) == slot_col).astype(F32)
     insert = jnp.concatenate([insert] * 3, axis=0).astype(BF16)
     length_col = jnp.sum(
@@ -228,27 +235,74 @@
         sum(out_blocks[a] * pre_ends[a * 4 + b : a * 4 + b + 1] for a in range(4)) for b in range(4)
     ]
 
-    start = jnp.where(active[None], right[...], 0.0)
-    basis[0] = start
-    end_values = [ends_of(start)]
-
-    def post(step, balance):
-        sends[step, 0, 0:4] = balance
-        sends[step, 1, 0:4] = pltpu.roll(balance, 32, 1)
+    to_table = (slot_of_junction_col == iota((128, 256), 1).astype(F32)).astype(F32).astype(BF16)
+
+    def stacked(value):
+        high = value.astype(BF16).astype(F32)
+        middle = (value - high).astype(BF16).astype(F32)
+        low = value - high - middle
+        return jnp.concatenate([high, middle, low, jnp.zeros_like(high)], axis=0).astype(BF16)
+
+    def unstacked(total):
+        return total[0:8] + total[8:16] + total[16:24]
+
+    def eight(value):
+        return jnp.concatenate([value, jnp.zeros_like(value)], axis=0)
+
+    def post(sends, recvs, near_rows, send_sem, recv_sem, balance, free):
+        table = unstacked(dot(stacked(eight(balance)), to_table))
+        for version in range(4):
+            shifted = pltpu.roll(table, 32 * version, 1) if version else table
+            sends[version, 0:4] = shifted[0:4, :128]
+            sends[version, 4:8] = shifted[0:4, 128:]
+            sends[version, 8:12] = pltpu.roll(free, 32, 1) if version % 2 else free
         copies = []
-        for index, offset in enumerate(o for o in range(-SPAN, SPAN + 1) if o != 0):
+        for offset in sorted(range(-FAR, FAR + 1), key=lambda o: -abs(o)):
+            if offset == 0:
+                continue
+            count = near_rows if abs(offset) <= SPAN else 8
             copy = pltpu.make_async_remote_copy(
-                src_ref=sends.at[step, offset % 2],
-                dst_ref=recvs.at[step, SPAN - offset],
-                send_sem=near_send.at[step, index],
-                recv_sem=near_recv.at[step, index],
+                src_ref=sends.at[-offset % 4, 0:count],
+                dst_ref=recvs.at[FAR - offset, 0:count],
+                send_sem=send_sem.at[FAR + offset],
+                recv_sem=recv_sem.at[FAR + offset],
                 device_id=near(offset),
                 device_id_type=MESH,
             )
             copy.start()
             copies.append(copy)
-        recvs[step, SPAN] = sends[step, 0]
+        recvs[FAR, 0:near_rows] = sends[0, 0:near_rows]
         return copies
+
+    def pieces(recvs, part):
+        joined = []
+        for index in range(0, PIECES, 2):
+            value = recvs[SPAN + index, part]
+            if index + 1 < PIECES:
+                value = value + recvs[SPAN + index + 1, part]
+            joined.append(value)
+        return joined
+
+    def balances(recvs, gather, frees, blocks, crosses, matches):
+        starts = []
+        for first in range(0, PEERS, 4):
+            total = recvs[first, 0:8]
+            for index in range(first + 1, min(first + 4, PEERS)):
+                total = total + recvs[index, 0:8]
+            starts.append(total)
+        table = [starts[k + 1] + pltpu.roll(starts[k], 4, 0) for k in range(4)]
+        left = stacked(jnp.concatenate(table, axis=1))
+        first = [
+            unstacked(dot(left[:, 128 * (j // 2) : 128 * (j // 2) + 256], gather[j]))[0:4]
+            for j in range(5)
+        ]
+        second = []
+        for j in range(5):
+            turned = pltpu.roll(first[j], 96, 1)
+            cross = apply(crosses[j], turned)
+            second.append(frees[j] + apply(blocks[j], first[j]) + pltpu.roll(cross, 96, 1))
+        own = dot(stacked(eight(jnp.concatenate(second, axis=1))), matches)
+        return first[2], unstacked(own)[0:4]
 
     def advance(step):
         if step == 0:
@@ -282,54 +336,81 @@
         total = jnp.sum(left * right_part, axis=(0, 1)).reshape(1, 256)
         return total[:, :128] + total[:, 128:]
 
-    balance = apply(to_balance, end_values[0])
-    sends[0, 0, 4:5] = jnp.maximum(id_row, 0).astype(F32)
-    sends[0, 1, 4:5] = pltpu.roll(jnp.maximum(id_row, 0).astype(F32), 32, 1)
+    def gram_rows(last, first_pair, last_pair):
+        for index, (i, j) in enumerate(PAIRS[first_pair:last_pair], first_pair):
+            gram_own[0, index : index + 1] = inner(last[i], last[j])
+
+    half = (lane & 32) == 0
+    pack = []
+    for a in range(4):
+        turned = pltpu.roll(in_blocks[a], 64, 1)
+        own = apply(to_balance, in_blocks[a])
+        cross = single * apply(to_balance, turned)
+        pack.append(own + pltpu.roll(cross, 32, 1))
+    pack = jnp.concatenate(pack, axis=0)
+    place_row = jnp.where((lane & 32) == 0, slot_of_junction_row + 1.0, 0.0)
+    for version in range(4):
+        turn = 32 * (version % 2)
+        sends_one[version, 12:13] = pltpu.roll(place_row, turn, 1) if turn else place_row
+        sends_one[version, 16:32] = pltpu.roll(pack, turn, 1) if turn else pack
+
+    start = jnp.where(active[None], right[...], 0.0)
+    basis[0] = start
+    balance = apply(to_balance, ends_of(start))
+    advance(0)
+    free = apply(to_balance, ends_of(bulk[...]))
     pl.semaphore_wait(barrier, len(partners))
-
-    pending = []
-    matches = None
-    for step in range(ITERS):
-        copies = post(step, balance)
-        pending += copies
-        advance(step)
-        bulk_ends = ends_of(bulk[...])
-        if step == ITERS - 1:
-            for index, (i, j) in enumerate(PAIRS):
-                other = bulk[...] if j == ITERS else basis[j]
-                value = bulk[...] if i == ITERS else basis[i]
-                gram_own[0, index : index + 1] = inner(value, other)
-            gram_own[0, len(PAIRS) : GRAM_ROWS] = jnp.zeros((GRAM_ROWS - len(PAIRS), 128), F32)
-        for copy in copies:
-            copy.wait_recv()
-        joined = jnp.concatenate(
-            [
-                recvs[step, index] + recvs[step, index + 1]
-                if index + 1 < PIECES
-                else recvs[step, index]
-                for index in range(0, PIECES, 2)
-            ],
-            axis=1,
-        )
-        if step == 0:
-            matches = (id_col == joined[4:5]).astype(F32).T.astype(BF16)
-        high = joined.astype(BF16).astype(F32)
-        middle = (joined - high).astype(BF16).astype(F32)
-        left = jnp.concatenate([high, middle, joined - high - middle, jnp.zeros_like(high)], axis=0)
-        sums = dot(left.astype(BF16), matches)
-        sums = sums[0:4] + sums[8:12] + sums[16:20]
-        added = apply(in_blocks, sums)
-        both = added + single * pltpu.roll(added, 64, 1)
-        if step < ITERS - 1:
-            end_values.append(bulk_ends + both)
-            balance = apply(to_balance, end_values[-1])
-            basis[step + 1] = bulk[...] + at_ends(added)
-        else:
-            for index, (i, j) in enumerate(PAIRS):
-                if j == ITERS:
-                    weight = 2.0 * bulk_ends + both if i == ITERS else end_values[i]
-                    row_sum = jnp.sum(weight * added, axis=0, keepdims=True)
-                    gram_own[0, index : index + 1] = gram_own[0, index : index + 1] + row_sum
+    copies = post(sends_one, recvs_one, 32, near_send.at[0], near_recv.at[0], balance, free)
+    pending = list(copies)
+    for copy in copies:
+        copy.wait_recv()
+
+    joined = pieces(recvs_one, slice(8, 16))
+    gather = []
+    place_rows = []
+    for j in range(5):
+        tagged = joined[j][4:5]
+        column = 2.0 * j + jnp.where(half, 0.0, 1.0)
+        position = jnp.where(tagged > 0.5, tagged - 1.0 + 32.0 * column, -1000.0)
+        place_rows.append(position)
+        rows_of = iota((256, 128), 0).astype(F32) + 128.0 * (j // 2)
+        gather.append((rows_of == position).astype(F32).astype(BF16))
+    own_place = jnp.where(slot_of_junction_col < 0.0, -2000.0, slot_of_junction_col + 128.0)
+    matches = (own_place == jnp.concatenate(place_rows, axis=1)).astype(F32).T.astype(BF16)
+    blocks = []
+    crosses = []
+    for index in range(0, PIECES, 2):
+        even = recvs_one[SPAN + index, 16:32]
+        odd = recvs_one[SPAN + index + 1, 16:32] if index + 1 < PIECES else jnp.zeros_like(even)
+        own = jnp.where(half, even, odd)
+        cross = jnp.where(half, odd, even)
+        blocks.append([own[4 * a : 4 * a + 4] for a in range(4)])
+        crosses.append([cross[4 * a : 4 * a + 4] for a in range(4)])
+
+    first, second = balances(
+        recvs_one, gather, [value[0:4] for value in joined], blocks, crosses, matches
+    )
+    basis[1] = bulk[...] + at_ends(apply(in_blocks, first))
+    advance(1)
+    basis[2] = bulk[...] + at_ends(apply(in_blocks, second))
+    balance = apply(to_balance, ends_of(basis[2]))
+    advance(2)
+    free = apply(to_balance, ends_of(bulk[...]))
+    copies = post(sends_two, recvs_two, 16, near_send.at[1], near_recv.at[1], balance, free)
+    pending += copies
+    gram_rows(basis, 0, 6)
+    gram_own[0, len(PAIRS) : GRAM_ROWS] = jnp.zeros((GRAM_ROWS - len(PAIRS), 128), F32)
+    for copy in copies:
+        copy.wait_recv()
+
+    joined = pieces(recvs_two, slice(8, 16))
+    first, second = balances(
+        recvs_two, gather, [value[0:4] for value in joined], blocks, crosses, matches
+    )
+    basis[3] = bulk[...] + at_ends(apply(in_blocks, first))
+    advance(3)
+    basis[4] = bulk[...] + at_ends(apply(in_blocks, second))
+    gram_rows(basis, 6, len(PAIRS))
 
     def all_sum(own, box, mine, member, count, send, recv):
         copies = []
@@ -363,17 +444,11 @@
     pending += copies
     gram = {pair: total[:, index : index + 1] for index, pair in enumerate(PAIRS)}
     coeffs = krylov_coeffs(gram)
-    stores = []
     for a in range(4):
         value = coeffs[0] * image[0, a]
         for k in range(1, ITERS):
             value = value + coeffs[k] * image[k, a]
         result[a] = value
-        store = pltpu.make_async_copy(result.at[a], result_hbm.at[a], out_sems.at[a])
-        store.start()
-        stores.append(store)
-    for store in stores:
-        store.wait()
     for copy in pending:
         copy.wait_send()
 
@@ -382,38 +457,38 @@
     pipes, slots = right_side.shape[1:]
     length = length.reshape(1, pipes)
     operands = (right_side, diag, lower, upper, precond, jout, jin, junction, length)
+    held = [pltpu.with_memory_space_constraint(value, pltpu.HBM) for value in operands]
     inputs = [pltpu.VMEM(value.shape, value.dtype) for value in operands]
     count_one, count_two = 2 * rows, columns // 2
-    near_count = PIECES - 1
     return pl.pallas_call(
         functools.partial(kernel, rows, columns),
-        out_shape=jax.ShapeDtypeStruct(right_side.shape, F32),
-        in_specs=[pl.BlockSpec(memory_space=pl.ANY)] * len(operands),
-        out_specs=pl.BlockSpec(memory_space=pl.ANY),
+        out_shape=pltpu.VMEM(right_side.shape, F32),
+        in_specs=[pl.BlockSpec(memory_space=pltpu.HBM)] * len(operands),
+        out_specs=pl.BlockSpec(memory_space=pltpu.VMEM),
         scratch_shapes=inputs
         + [
-            pltpu.VMEM((ITERS, 4, pipes, slots), F32),
+            pltpu.VMEM((ITERS + 1, 4, pipes, slots), F32),
             pltpu.VMEM((ITERS, 4, pipes, slots), F32),
             pltpu.VMEM((4, pipes, slots), F32),
-            pltpu.VMEM((4, pipes, slots), F32),
-            pltpu.VMEM((ITERS, 2, 8, 128), F32),
-            pltpu.VMEM((ITERS, PIECES, 8, 128), F32),
+            pltpu.VMEM((4, 32, 128), F32),
+            pltpu.VMEM((4, 16, 128), F32),
+            pltpu.VMEM((PEERS, 32, 128), F32),
+            pltpu.VMEM((PEERS, 16, 128), F32),
             pltpu.VMEM((2, GRAM_ROWS, 128), F32),
             pltpu.VMEM((count_one, 1, 128), F32),
             pltpu.VMEM((count_two, 1, 128), F32),
             pltpu.SemaphoreType.DMA((len(operands),)),
-            pltpu.SemaphoreType.DMA((4,)),
-            pltpu.SemaphoreType.DMA((ITERS, near_count)),
-            pltpu.SemaphoreType.DMA((ITERS, near_count)),
+            pltpu.SemaphoreType.DMA((2, PEERS)),
+            pltpu.SemaphoreType.DMA((2, PEERS)),
             pltpu.SemaphoreType.DMA((count_one,)),
             pltpu.SemaphoreType.DMA((count_one,)),
             pltpu.SemaphoreType.DMA((count_two,)),
             pltpu.SemaphoreType.DMA((count_two,)),
         ],
         compiler_params=pltpu.CompilerParams(
-            collective_id=0, has_side_effects=True, vmem_limit_bytes=63 * 1024 * 1024
+            collective_id=0, has_side_effects=True, vmem_limit_bytes=48 * 1024 * 1024
         ),
-    )(*operands)
+    )(*held)
 
 
 def solution(mesh):

time: 42 us -> 33.8 us (0.80)
  Pallas kernels: 40.3 us -> 33.1 us
  local copies, waits for them, and re-layouts: 1.57 us -> 0.66 us
    pallas_call x1, Pallas kernels: 40.3 us -> 33.1 us  [body(): pl.pallas_call(functools.partial(kernel, rows, columns), out_shape=pltpu....]
    unnamed x1, local copies, waits for them, and re-layouts: 1.57 us -> 0.66 us
where the time goes in v3:
time: 33.8 us; the launch traced here: 33.7 us
  Pallas kernels  33.1 us (98%)
  local copies, waits for them, and re-layouts  0.66 us (2%)
    pallas_call x1, Pallas kernels, body(): pl.pallas_call(functools.partial(kernel, rows, columns), out_shape=pltpu....  33.1 us

profile of v3, /device:TPU:1, one launch (start us, length us, event | category | flops | bytes accessed | tf_op | source)
XLA Modules:
  0.0 33.7 jit_solution(8214534070060109710)
XLA Ops:
  0.0 33.1 %shard_map.91 = f32[4,32,256]{2,1,0:T(8,128)S(1)} custom-call(f32[4,32,256]{2,1,0:T(8,128)} %right_hbm.1, bf16[4,4,32,256]{3,2,1,0:T(8,128)(2,1)} %diag_hbm.1, bf16[4,4,32,256]{3,2,1,0:T(8,128)(2,1)} %lower_hbm.1, bf16[4,4,32,256]{3,2,1,0:T(8,128)(2,1)} %upper_hbm.1, bf16[4,4,32,256]{3,2,1,0:T(8,128)(2,1)} %precond_hbm.1, f32[2,4,4,32]{3,2,1,0:T(4,128)} %out_hbm_blocks.1, ...), custom_call_target="tpu_custom_call" | custom-call | tf_op jit(solution)/shard_map/pallas_call | solution.py:463
  33.1 0.7 %copy.11 = f32[4,32,256]{2,1,0:T(8,128)} copy(f32[4,32,256]{2,1,0:T(8,128)S(1)} %shard_map.91) | data formatting | bytes 262144

commit v4 on v3

--- a/solution.py
+++ b/solution.py
@@ -46,15 +46,16 @@
     target = [beta] + [None] * steps
     cosines = []
     sines = []
+    inverses = []
     for k in range(steps):
         for i in range(k):
             temp = cosines[i] * upper[i][k] + sines[i] * upper[i + 1][k]
-            upper[i + 1][k] = -sines[i] * upper[i][k] + cosines[i] * upper[i + 1][k]
+            upper[i + 1][k] = cosines[i] * upper[i + 1][k] - sines[i] * upper[i][k]
             upper[i][k] = temp
-        inverse = 1.0 / jnp.sqrt(upper[k][k] * upper[k][k] + upper[k + 1][k] * upper[k + 1][k])
+        inverse = lax.rsqrt(upper[k][k] * upper[k][k] + upper[k + 1][k] * upper[k + 1][k])
         cosines.append(upper[k][k] * inverse)
         sines.append(upper[k + 1][k] * inverse)
-        upper[k][k] = cosines[k] * upper[k][k] + sines[k] * upper[k + 1][k]
+        inverses.append(inverse)
         target[k + 1] = -sines[k] * target[k]
         target[k] = cosines[k] * target[k]
     coeffs = [None] * steps
@@ -62,7 +63,7 @@
         total = target[k]
         for j in range(k + 1, steps):
             total = total - upper[k][j] * coeffs[j]
-        coeffs[k] = total / upper[k][k]
+        coeffs[k] = total * inverses[k]
     return coeffs
 
 
@@ -121,38 +122,26 @@
     bulk,
     sends_one,
     sends_two,
+    block_sends,
     recvs_one,
     recvs_two,
+    block_recvs,
     gram_own,
-    gram_one,
-    gram_two,
+    gram_row,
+    gram_all,
     in_sems,
     near_send,
     near_recv,
-    one_send,
-    one_recv,
-    two_send,
-    two_recv,
+    block_send,
+    block_recv,
+    all_send,
+    all_recv,
 ):
     row = lax.axis_index("row")
     col = lax.axis_index("col")
-    count_one = 2 * rows
-    count_two = columns // 2
-    core = col % 2
-    place = col // 2
-    mine_one = row * 2 + core
-    mine_two = place
 
     def near(offset):
         return (row, (col + offset + columns) % columns)
-
-    def member_one(step):
-        index = (mine_one + step) % count_one
-        return (index // 2, place * 2 + index % 2)
-
-    def member_two(step):
-        index = (mine_two + step) % count_two
-        return (row, index * 2 + core)
 
     loads = [
         pltpu.make_async_copy(source, target, in_sems.at[index])
@@ -174,9 +163,8 @@
         load.start()
 
     barrier = pltpu.get_barrier_semaphore()
-    partners = [near(offset) for offset in range(1 - FAR, FAR, 2)]
-    partners += [member_one(step) for step in range(1, count_one)]
-    partners += [member_two(step) for step in range(1, count_two)]
+    partners = [near(offset) for offset in range(-FAR, FAR + 1) if offset != 0]
+    partners += [((row + step) % rows, col) for step in range(1, rows)]
     for partner in partners:
         pl.semaphore_signal(barrier, inc=1, device_id=partner, device_id_type=MESH)
 
@@ -283,7 +271,7 @@
             joined.append(value)
         return joined
 
-    def balances(recvs, gather, frees, blocks, crosses, matches):
+    def near_balances(recvs, gather):
         starts = []
         for first in range(0, PEERS, 4):
             total = recvs[first, 0:8]
@@ -292,17 +280,19 @@
             starts.append(total)
         table = [starts[k + 1] + pltpu.roll(starts[k], 4, 0) for k in range(4)]
         left = stacked(jnp.concatenate(table, axis=1))
-        first = [
+        return [
             unstacked(dot(left[:, 128 * (j // 2) : 128 * (j // 2) + 256], gather[j]))[0:4]
             for j in range(5)
         ]
+
+    def next_balances(first, frees, blocks, crosses, matches):
         second = []
         for j in range(5):
             turned = pltpu.roll(first[j], 96, 1)
             cross = apply(crosses[j], turned)
             second.append(frees[j] + apply(blocks[j], first[j]) + pltpu.roll(cross, 96, 1))
         own = dot(stacked(eight(jnp.concatenate(second, axis=1))), matches)
-        return first[2], unstacked(own)[0:4]
+        return unstacked(own)[0:4]
 
     def advance(step):
         if step == 0:
@@ -352,7 +342,8 @@
     for version in range(4):
         turn = 32 * (version % 2)
         sends_one[version, 12:13] = pltpu.roll(place_row, turn, 1) if turn else place_row
-        sends_one[version, 16:32] = pltpu.roll(pack, turn, 1) if turn else pack
+    block_sends[0] = pack
+    block_sends[1] = pltpu.roll(pack, 32, 1)
 
     start = jnp.where(active[None], right[...], 0.0)
     basis[0] = start
@@ -360,12 +351,26 @@
     advance(0)
     free = apply(to_balance, ends_of(bulk[...]))
     pl.semaphore_wait(barrier, len(partners))
-    copies = post(sends_one, recvs_one, 32, near_send.at[0], near_recv.at[0], balance, free)
-    pending = list(copies)
+    copies = post(sends_one, recvs_one, 13, near_send.at[0], near_recv.at[0], balance, free)
+    block_copies = []
+    for offset in sorted(range(-SPAN, SPAN + 1), key=lambda o: -abs(o)):
+        if offset != 0:
+            copy = pltpu.make_async_remote_copy(
+                src_ref=block_sends.at[offset % 2],
+                dst_ref=block_recvs.at[SPAN - offset],
+                send_sem=block_send.at[SPAN + offset],
+                recv_sem=block_recv.at[SPAN + offset],
+                device_id=near(offset),
+                device_id_type=MESH,
+            )
+            copy.start()
+            block_copies.append(copy)
+    block_recvs[SPAN] = block_sends[0]
+    pending = copies + block_copies
     for copy in copies:
         copy.wait_recv()
 
-    joined = pieces(recvs_one, slice(8, 16))
+    joined = pieces(recvs_one, slice(8, 13))
     gather = []
     place_rows = []
     for j in range(5):
@@ -377,80 +382,80 @@
         gather.append((rows_of == position).astype(F32).astype(BF16))
     own_place = jnp.where(slot_of_junction_col < 0.0, -2000.0, slot_of_junction_col + 128.0)
     matches = (own_place == jnp.concatenate(place_rows, axis=1)).astype(F32).T.astype(BF16)
+    first = near_balances(recvs_one, gather)
+    for copy in block_copies:
+        copy.wait_recv()
     blocks = []
     crosses = []
     for index in range(0, PIECES, 2):
-        even = recvs_one[SPAN + index, 16:32]
-        odd = recvs_one[SPAN + index + 1, 16:32] if index + 1 < PIECES else jnp.zeros_like(even)
+        even = block_recvs[index]
+        odd = block_recvs[index + 1] if index + 1 < PIECES else jnp.zeros_like(even)
         own = jnp.where(half, even, odd)
         cross = jnp.where(half, odd, even)
         blocks.append([own[4 * a : 4 * a + 4] for a in range(4)])
         crosses.append([cross[4 * a : 4 * a + 4] for a in range(4)])
 
-    first, second = balances(
-        recvs_one, gather, [value[0:4] for value in joined], blocks, crosses, matches
-    )
-    basis[1] = bulk[...] + at_ends(apply(in_blocks, first))
+    second = next_balances(first, [value[0:4] for value in joined], blocks, crosses, matches)
+    basis[1] = bulk[...] + at_ends(apply(in_blocks, first[2]))
     advance(1)
     basis[2] = bulk[...] + at_ends(apply(in_blocks, second))
     balance = apply(to_balance, ends_of(basis[2]))
     advance(2)
     free = apply(to_balance, ends_of(bulk[...]))
-    copies = post(sends_two, recvs_two, 16, near_send.at[1], near_recv.at[1], balance, free)
+    copies = post(sends_two, recvs_two, 12, near_send.at[1], near_recv.at[1], balance, free)
     pending += copies
     gram_rows(basis, 0, 6)
     gram_own[0, len(PAIRS) : GRAM_ROWS] = jnp.zeros((GRAM_ROWS - len(PAIRS), 128), F32)
     for copy in copies:
         copy.wait_recv()
 
-    joined = pieces(recvs_two, slice(8, 16))
-    first, second = balances(
-        recvs_two, gather, [value[0:4] for value in joined], blocks, crosses, matches
-    )
-    basis[3] = bulk[...] + at_ends(apply(in_blocks, first))
+    joined = pieces(recvs_two, slice(8, 12))
+    first = near_balances(recvs_two, gather)
+    second = next_balances(first, joined, blocks, crosses, matches)
+    basis[3] = bulk[...] + at_ends(apply(in_blocks, first[2]))
     advance(3)
     basis[4] = bulk[...] + at_ends(apply(in_blocks, second))
     gram_rows(basis, 6, len(PAIRS))
 
-    def all_sum(own, box, mine, member, count, send, recv):
-        copies = []
-        for step in range(1, count):
-            copy = pltpu.make_async_remote_copy(
-                src_ref=own,
-                dst_ref=box.at[mine],
-                send_sem=send.at[step],
-                recv_sem=recv.at[step],
-                device_id=member(step),
-                device_id_type=MESH,
-            )
-            copy.start()
-            copies.append(copy)
-        box[mine] = own[...]
-        for copy in copies:
-            copy.wait_recv()
-        return copies, jnp.sum(box[...], axis=0)
-
     partial = jnp.sum(gram_own[0], axis=1, keepdims=True)
     eye = iota((GRAM_ROWS, 128), 0) == iota((GRAM_ROWS, 128), 1)
-    gram_own[1, 0:1] = jnp.sum(jnp.where(eye, partial, 0.0), axis=0, keepdims=True)
-    copies, total = all_sum(
-        gram_own.at[1, 0:1], gram_one, mine_one, member_one, count_one, one_send, one_recv
-    )
-    pending += copies
-    gram_own[1, 8:9] = total
-    copies, total = all_sum(
-        gram_own.at[1, 8:9], gram_two, mine_two, member_two, count_two, two_send, two_recv
-    )
-    pending += copies
-    gram = {pair: total[:, index : index + 1] for index, pair in enumerate(PAIRS)}
-    coeffs = krylov_coeffs(gram)
+    mine = row * columns + col
+    gram_row[0] = jnp.sum(jnp.where(eye, partial, 0.0), axis=0, keepdims=True)
+    gram_all[mine] = gram_row[0]
+    others = rows * columns - 1
+
+    def tell(index, carry):
+        target = index + jnp.where(index >= mine, 1, 0)
+        pltpu.make_async_remote_copy(
+            src_ref=gram_row.at[0],
+            dst_ref=gram_all.at[mine],
+            send_sem=all_send,
+            recv_sem=all_recv,
+            device_id=(target // columns, target % columns),
+            device_id_type=MESH,
+        ).start()
+        return carry
+
+    lax.fori_loop(0, others, tell, 0, unroll=5)
+    received = gram_all.at[0:others]
+    pltpu.make_async_copy(received, received, all_recv).wait()
+    total = jnp.sum(gram_all[...], axis=0)
+    splat = jnp.sum(jnp.where(eye, total, 0.0), axis=1, keepdims=True)
+    splat = jnp.broadcast_to(splat, (GRAM_ROWS, 128))
+    gram = {
+        pair: jnp.broadcast_to(splat[index : index + 1], (8, 128))
+        for index, pair in enumerate(PAIRS)
+    }
+    coeffs = [jnp.broadcast_to(value[0:1], (32, 128)) for value in krylov_coeffs(gram)]
     for a in range(4):
-        value = coeffs[0] * image[0, a]
-        for k in range(1, ITERS):
-            value = value + coeffs[k] * image[k, a]
-        result[a] = value
+        for lanes in (slice(0, 128), slice(128, 256)):
+            value = coeffs[0] * image[0, a, :, lanes]
+            for k in range(1, ITERS):
+                value = value + coeffs[k] * image[k, a, :, lanes]
+            result[a, :, lanes] = value
     for copy in pending:
         copy.wait_send()
+    pltpu.make_async_copy(received, received, all_send).wait()
 
 
 def body(rows, columns, right_side, diag, lower, upper, precond, jout, jin, junction, length):
@@ -459,7 +464,6 @@
     operands = (right_side, diag, lower, upper, precond, jout, jin, junction, length)
     held = [pltpu.with_memory_space_constraint(value, pltpu.HBM) for value in operands]
     inputs = [pltpu.VMEM(value.shape, value.dtype) for value in operands]
-    count_one, count_two = 2 * rows, columns // 2
     return pl.pallas_call(
         functools.partial(kernel, rows, columns),
         out_shape=pltpu.VMEM(right_side.shape, F32),
@@ -470,20 +474,22 @@
             pltpu.VMEM((ITERS + 1, 4, pipes, slots), F32),
             pltpu.VMEM((ITERS, 4, pipes, slots), F32),
             pltpu.VMEM((4, pipes, slots), F32),
-            pltpu.VMEM((4, 32, 128), F32),
             pltpu.VMEM((4, 16, 128), F32),
-            pltpu.VMEM((PEERS, 32, 128), F32),
+            pltpu.VMEM((4, 16, 128), F32),
+            pltpu.VMEM((2, 16, 128), F32),
             pltpu.VMEM((PEERS, 16, 128), F32),
-            pltpu.VMEM((2, GRAM_ROWS, 128), F32),
-            pltpu.VMEM((count_one, 1, 128), F32),
-            pltpu.VMEM((count_two, 1, 128), F32),
+            pltpu.VMEM((PEERS, 16, 128), F32),
+            pltpu.VMEM((PIECES, 16, 128), F32),
+            pltpu.VMEM((1, GRAM_ROWS, 128), F32),
+            pltpu.VMEM((1, 1, 128), F32),
+            pltpu.VMEM((rows * columns, 1, 128), F32),
             pltpu.SemaphoreType.DMA((len(operands),)),
             pltpu.SemaphoreType.DMA((2, PEERS)),
             pltpu.SemaphoreType.DMA((2, PEERS)),
-            pltpu.SemaphoreType.DMA((count_one,)),
-            pltpu.SemaphoreType.DMA((count_one,)),
-            pltpu.SemaphoreType.DMA((count_two,)),
-            pltpu.SemaphoreType.DMA((count_two,)),
+            pltpu.SemaphoreType.DMA((PIECES,)),
+            pltpu.SemaphoreType.DMA((PIECES,)),
+            pltpu.SemaphoreType.DMA,
+            pltpu.SemaphoreType.DMA,
         ],
         compiler_params=pltpu.CompilerParams(
             collective_id=0, has_side_effects=True, vmem_limit_bytes=48 * 1024 * 1024

time: 33.8 us -> 30.5 us (0.902)
  Pallas kernels: 33.1 us -> 29.8 us
    pallas_call x1, Pallas kernels: 33.1 us -> 29.8 us  [body(): pl.pallas_call(functools.partial(kernel, rows, columns), out_shape=pltpu....]
where the time goes in v4:
time: 30.5 us; the launch traced here: 30.4 us
  Pallas kernels  29.8 us (98%)
  local copies, waits for them, and re-layouts  0.66 us (2%)
    pallas_call x1, Pallas kernels, body(): pl.pallas_call(functools.partial(kernel, rows, columns), out_shape=pltpu....  29.8 us
    unnamed x1, local copies, waits for them, and re-layouts  0.66 us

profile of v4, /device:TPU:1, one launch (start us, length us, event | category | flops | bytes accessed | tf_op | source)
XLA Modules:
  0.0 30.4 jit_solution(7990097540909528321)
XLA Ops:
  0.0 29.8 %shard_map.91 = f32[4,32,256]{2,1,0:T(8,128)S(1)} custom-call(f32[4,32,256]{2,1,0:T(8,128)} %right_hbm.1, bf16[4,4,32,256]{3,2,1,0:T(8,128)(2,1)} %diag_hbm.1, bf16[4,4,32,256]{3,2,1,0:T(8,128)(2,1)} %lower_hbm.1, bf16[4,4,32,256]{3,2,1,0:T(8,128)(2,1)} %upper_hbm.1, bf16[4,4,32,256]{3,2,1,0:T(8,128)(2,1)} %precond_hbm.1, f32[2,4,4,32]{3,2,1,0:T(4,128)} %out_hbm_blocks.1, ...), custom_call_target="tpu_custom_call" | custom-call | tf_op jit(solution)/shard_map/pallas_call | solution.py:467
  29.8 0.7 %copy.11 = f32[4,32,256]{2,1,0:T(8,128)} copy(f32[4,32,256]{2,1,0:T(8,128)S(1)} %shard_map.91) | data formatting | bytes 262144

commit v5 on v4

--- a/solution.py
+++ b/solution.py
@@ -120,6 +120,7 @@
     basis,
     image,
     bulk,
+    spare,
     sends_one,
     sends_two,
     block_sends,
@@ -143,6 +144,12 @@
     def near(offset):
         return (row, (col + offset + columns) % columns)
 
+    barrier = pltpu.get_barrier_semaphore()
+    partners = [near(offset) for offset in range(-FAR, FAR + 1) if offset != 0]
+    partners += [((row + step) % rows, col) for step in range(1, rows)]
+    for partner in partners:
+        pl.semaphore_signal(barrier, inc=1, device_id=partner, device_id_type=MESH)
+
     loads = [
         pltpu.make_async_copy(source, target, in_sems.at[index])
         for index, (source, target) in enumerate(
@@ -162,15 +169,9 @@
     for load in loads:
         load.start()
 
-    barrier = pltpu.get_barrier_semaphore()
-    partners = [near(offset) for offset in range(-FAR, FAR + 1) if offset != 0]
-    partners += [((row + step) % rows, col) for step in range(1, rows)]
-    for partner in partners:
-        pl.semaphore_signal(barrier, inc=1, device_id=partner, device_id_type=MESH)
-
     sends_one[...] = jnp.zeros_like(sends_one)
     sends_two[...] = jnp.zeros_like(sends_two)
-    for load in loads[:6]:
+    for load in loads[:2]:
         load.wait()
 
     lane = iota((1, 128), 1)
@@ -215,12 +216,20 @@
             total = total + blocks[a] * value[a : a + 1]
         return total
 
+    for load in loads[2:6]:
+        load.wait()
     out_blocks = [block_row(jout, a) for a in range(4)]
     in_blocks = [block_row(jin, a) for a in range(4)]
-    pre_ends = dot(precond[...].reshape(512, 256), extract).reshape(16, 32, 128)
-    pre_ends = jnp.sum(jnp.where(own_pipe, pre_ends, 0.0), axis=1)
+
+    def block_ends(blocks, at):
+        total = dot(blocks, at).reshape(16, 32, 128)
+        total = jnp.sum(jnp.where(own_pipe, total, 0.0), axis=1)
+        return [total[4 * a : 4 * a + 4] for a in range(4)]
+
+    pre_blocks = jnp.concatenate([precond[a, b] for b in range(4) for a in range(4)], axis=0)
+    pre_ends = block_ends(pre_blocks, extract)
     to_balance = [
-        sum(out_blocks[a] * pre_ends[a * 4 + b : a * 4 + b + 1] for a in range(4)) for b in range(4)
+        sum(out_blocks[a] * pre_ends[b][a : a + 1] for a in range(4)) for b in range(4)
     ]
 
     to_table = (slot_of_junction_col == iota((128, 256), 1).astype(F32)).astype(F32).astype(BF16)
@@ -237,13 +246,15 @@
     def eight(value):
         return jnp.concatenate([value, jnp.zeros_like(value)], axis=0)
 
-    def post(sends, recvs, near_rows, send_sem, recv_sem, balance, free):
+    def fill(sends, balance, free):
         table = unstacked(dot(stacked(eight(balance)), to_table))
         for version in range(4):
             shifted = pltpu.roll(table, 32 * version, 1) if version else table
             sends[version, 0:4] = shifted[0:4, :128]
             sends[version, 4:8] = shifted[0:4, 128:]
             sends[version, 8:12] = pltpu.roll(free, 32, 1) if version % 2 else free
+
+    def post(sends, recvs, near_rows, send_sem, recv_sem):
         copies = []
         for offset in sorted(range(-FAR, FAR + 1), key=lambda o: -abs(o)):
             if offset == 0:
@@ -294,19 +305,17 @@
         own = dot(stacked(eight(jnp.concatenate(second, axis=1))), matches)
         return unstacked(own)[0:4]
 
-    def advance(step):
-        if step == 0:
-            for load in loads[6:]:
-                load.wait()
+    def advance(source, target, picture=None):
         for first in range(0, 32, CHUNK):
             part = slice(first, first + CHUNK)
-            vec = [basis[step, b, part] for b in range(4)]
+            vec = [source[b, part] for b in range(4)]
             x = []
             for a in range(4):
                 total = precond[a, 0, part].astype(F32) * vec[0]
                 for b in range(1, 4):
                     total = total + precond[a, b, part].astype(F32) * vec[b]
-                image[step, a, part] = total
+                if picture is not None:
+                    picture[a, part] = total
                 x.append(total)
             keep = active[part]
             slot = iota((CHUNK, 256), 1)
@@ -320,7 +329,7 @@
                 following = jnp.where(slot == 255, 0.0, pltpu.roll(sums[1], 255, 1))
                 preceding = jnp.where(slot == 0, 0.0, pltpu.roll(sums[2], 1, 1))
                 total = jnp.where(keep, sums[0] + following + preceding, 0.0)
-                bulk[b, part] = total - SHIFT * vec[b]
+                target[b, part] = total - SHIFT * vec[b]
 
     def inner(left, right_part):
         total = jnp.sum(left * right_part, axis=(0, 1)).reshape(1, 256)
@@ -348,10 +357,14 @@
     start = jnp.where(active[None], right[...], 0.0)
     basis[0] = start
     balance = apply(to_balance, ends_of(start))
-    advance(0)
-    free = apply(to_balance, ends_of(bulk[...]))
+    for load in loads[6:]:
+        load.wait()
+    advance(basis.at[0], bulk, image.at[0])
+    bulk_ends = ends_of(bulk[...])
+    free = apply(to_balance, bulk_ends)
+    fill(sends_one, balance, free)
     pl.semaphore_wait(barrier, len(partners))
-    copies = post(sends_one, recvs_one, 13, near_send.at[0], near_recv.at[0], balance, free)
+    copies = post(sends_one, recvs_one, 13, near_send.at[0], near_recv.at[0])
     block_copies = []
     for offset in sorted(range(-SPAN, SPAN + 1), key=lambda o: -abs(o)):
         if offset != 0:
@@ -367,6 +380,54 @@
             block_copies.append(copy)
     block_recvs[SPAN] = block_sends[0]
     pending = copies + block_copies
+
+    advance(bulk, spare.at[0])
+    spare_ends = ends_of(spare[0])
+    advance(spare.at[0], spare.at[1])
+    far_ends = ends_of(spare[1])
+    is_first = lane < 64
+    used = (lane & 32) == 0
+    extracts = [extract]
+    for depth in (1, 2):
+        slot = jnp.where(is_first, depth, length_row - 1 - depth)
+        slot = jnp.where(used & (length_row > depth), slot, -1)
+        extracts.append((iota((256, 128), 0) == slot).astype(F32).astype(BF16))
+    pre_at = [pre_ends] + [block_ends(pre_blocks, extracts[d]) for d in (1, 2)]
+    diag_at = [block_ends(diag[...].reshape(512, 256), extracts[d]) for d in (0, 1)]
+    lower_at = [block_ends(lower[...].reshape(512, 256), extracts[d]) for d in range(3)]
+    upper_at = [block_ends(upper[...].reshape(512, 256), extracts[d]) for d in range(3)]
+    inward = [None] + [
+        [jnp.where(is_first, lower_at[d][a], upper_at[d][a]) for a in range(4)] for d in (1, 2)
+    ]
+    outward = [
+        [
+            jnp.where(
+                length_row > d + 1, jnp.where(is_first, upper_at[d][a], lower_at[d][a]), 0.0
+            )
+            for a in range(4)
+        ]
+        for d in (0, 1)
+    ]
+    of_length = [((length_row == count) & used).astype(F32) for count in (1, 2, 3)]
+
+    def at_depths(added):
+        other = pltpu.roll(added, 64, 1)
+        return [added + of_length[0] * other, of_length[1] * other, of_length[2] * other]
+
+    def step_at_end(value):
+        x = [apply(pre_at[d], value[d]) for d in (0, 1)]
+        return apply(diag_at[0], x[0]) + apply(inward[1], x[1]) - SHIFT * value[0]
+
+    def step_at_ends(value):
+        x = [apply(pre_at[d], value[d]) for d in range(3)]
+        return [
+            apply(diag_at[0], x[0]) + apply(inward[1], x[1]) - SHIFT * value[0],
+            apply(diag_at[1], x[1])
+            + apply(outward[0], x[0])
+            + apply(inward[2], x[2])
+            - SHIFT * value[1],
+        ]
+
     for copy in copies:
         copy.wait_recv()
 
@@ -396,14 +457,19 @@
         crosses.append([cross[4 * a : 4 * a + 4] for a in range(4)])
 
     second = next_balances(first, [value[0:4] for value in joined], blocks, crosses, matches)
-    basis[1] = bulk[...] + at_ends(apply(in_blocks, first[2]))
-    advance(1)
-    basis[2] = bulk[...] + at_ends(apply(in_blocks, second))
-    balance = apply(to_balance, ends_of(basis[2]))
-    advance(2)
-    free = apply(to_balance, ends_of(bulk[...]))
-    copies = post(sends_two, recvs_two, 12, near_send.at[1], near_recv.at[1], balance, free)
+    added_one = apply(in_blocks, first[2])
+    added_two = apply(in_blocks, second)
+    moved = step_at_ends(at_depths(added_one))
+    moved = [value + more for value, more in zip(moved, at_depths(added_two))]
+    balance = apply(to_balance, spare_ends + moved[0])
+    free = apply(to_balance, far_ends + step_at_end(moved))
+    fill(sends_two, balance, free)
+    copies = post(sends_two, recvs_two, 12, near_send.at[1], near_recv.at[1])
     pending += copies
+    basis[1] = bulk[...] + at_ends(added_one)
+    advance(basis.at[1], bulk, image.at[1])
+    basis[2] = bulk[...] + at_ends(added_two)
+    advance(basis.at[2], bulk, image.at[2])
     gram_rows(basis, 0, 6)
     gram_own[0, len(PAIRS) : GRAM_ROWS] = jnp.zeros((GRAM_ROWS - len(PAIRS), 128), F32)
     for copy in copies:
@@ -413,7 +479,7 @@
     first = near_balances(recvs_two, gather)
     second = next_balances(first, joined, blocks, crosses, matches)
     basis[3] = bulk[...] + at_ends(apply(in_blocks, first[2]))
-    advance(3)
+    advance(basis.at[3], bulk, image.at[3])
     basis[4] = bulk[...] + at_ends(apply(in_blocks, second))
     gram_rows(basis, 6, len(PAIRS))
 
@@ -425,13 +491,13 @@
     others = rows * columns - 1
 
     def tell(index, carry):
-        target = index + jnp.where(index >= mine, 1, 0)
+        target = index + jnp.where(index >= row * columns, 1, 0)
         pltpu.make_async_remote_copy(
             src_ref=gram_row.at[0],
             dst_ref=gram_all.at[mine],
             send_sem=all_send,
             recv_sem=all_recv,
-            device_id=(target // columns, target % columns),
+            device_id=(target // columns, (col + target) % columns),
             device_id_type=MESH,
         ).start()
         return carry
@@ -474,6 +540,7 @@
             pltpu.VMEM((ITERS + 1, 4, pipes, slots), F32),
             pltpu.VMEM((ITERS, 4, pipes, slots), F32),
             pltpu.VMEM((4, pipes, slots), F32),
+            pltpu.VMEM((2, 4, pipes, slots), F32),
             pltpu.VMEM((4, 16, 128), F32),
             pltpu.VMEM((4, 16, 128), F32),
             pltpu.VMEM((2, 16, 128), F32),

time: 30.5 us -> 29.9 us (0.980)
  Pallas kernels: 29.8 us -> 29.1 us
    pallas_call x1, Pallas kernels: 29.8 us -> 29.1 us  [body(): pl.pallas_call(functools.partial(kernel, rows, columns), out_shape=pltpu....]
where the time goes in v5:
time: 29.9 us; the launch traced here: 29.8 us
  Pallas kernels  29.1 us (97%)
  local copies, waits for them, and re-layouts  0.66 us (2%)
    pallas_call x1, Pallas kernels, body(): pl.pallas_call(functools.partial(kernel, rows, columns), out_shape=pltpu....  29.1 us
    unnamed x1, local copies, waits for them, and re-layouts  0.66 us

profile of v5, /device:TPU:1, one launch (start us, length us, event | category | flops | bytes accessed | tf_op | source)
XLA Modules:
  0.0 29.8 jit_solution(15380243852263722129)
XLA Ops:
  0.0 29.1 %shard_map.91 = f32[4,32,256]{2,1,0:T(8,128)S(1)} custom-call(f32[4,32,256]{2,1,0:T(8,128)} %right_hbm.1, bf16[4,4,32,256]{3,2,1,0:T(8,128)(2,1)} %diag_hbm.1, bf16[4,4,32,256]{3,2,1,0:T(8,128)(2,1)} %lower_hbm.1, bf16[4,4,32,256]{3,2,1,0:T(8,128)(2,1)} %upper_hbm.1, bf16[4,4,32,256]{3,2,1,0:T(8,128)(2,1)} %precond_hbm.1, f32[2,4,4,32]{3,2,1,0:T(4,128)} %out_hbm_blocks.1, ...), custom_call_target="tpu_custom_call" | custom-call | tf_op jit(solution)/shard_map/pallas_call | solution.py:533
  29.1 0.7 %copy.11 = f32[4,32,256]{2,1,0:T(8,128)} copy(f32[4,32,256]{2,1,0:T(8,128)S(1)} %shard_map.91) | data formatting | bytes 262144

commit v6 on v5

--- a/solution.py
+++ b/solution.py
@@ -199,8 +199,8 @@
     single = ((length_row == 1) & ((lane & 32) == 0)).astype(F32)
     own_pipe = (iota((32, 128), 0) == (iota((32, 128), 1) & 63))[None]
 
-    def ends_of(value):
-        total = sum(dot(part, extract) for part in split3(value.reshape(128, 256)))
+    def ends_of(value, at=extract):
+        total = sum(dot(part, at) for part in split3(value.reshape(128, 256)))
         return jnp.sum(jnp.where(own_pipe, total.reshape(4, 32, 128), 0.0), axis=1)
 
     def at_ends(value):
@@ -335,10 +335,6 @@
         total = jnp.sum(left * right_part, axis=(0, 1)).reshape(1, 256)
         return total[:, :128] + total[:, 128:]
 
-    def gram_rows(last, first_pair, last_pair):
-        for index, (i, j) in enumerate(PAIRS[first_pair:last_pair], first_pair):
-            gram_own[0, index : index + 1] = inner(last[i], last[j])
-
     half = (lane & 32) == 0
     pack = []
     for a in range(4):
@@ -356,7 +352,8 @@
 
     start = jnp.where(active[None], right[...], 0.0)
     basis[0] = start
-    balance = apply(to_balance, ends_of(start))
+    start_ends = ends_of(start)
+    balance = apply(to_balance, start_ends)
     for load in loads[6:]:
         load.wait()
     advance(basis.at[0], bulk, image.at[0])
@@ -461,8 +458,14 @@
     added_two = apply(in_blocks, second)
     moved = step_at_ends(at_depths(added_one))
     moved = [value + more for value, more in zip(moved, at_depths(added_two))]
-    balance = apply(to_balance, spare_ends + moved[0])
-    free = apply(to_balance, far_ends + step_at_end(moved))
+    ends_at = [
+        start_ends,
+        bulk_ends + at_depths(added_one)[0],
+        spare_ends + moved[0],
+        far_ends + step_at_end(moved),
+    ]
+    balance = apply(to_balance, ends_at[2])
+    free = apply(to_balance, ends_at[3])
     fill(sends_two, balance, free)
     copies = post(sends_two, recvs_two, 12, near_send.at[1], near_recv.at[1])
     pending += copies
@@ -470,20 +473,54 @@
     advance(basis.at[1], bulk, image.at[1])
     basis[2] = bulk[...] + at_ends(added_two)
     advance(basis.at[2], bulk, image.at[2])
-    gram_rows(basis, 0, 6)
+
+    advance(bulk, spare.at[0])
+    vectors = [basis.at[0], basis.at[1], basis.at[2], bulk, spare.at[0]]
+    for index, (i, j) in enumerate(PAIRS):
+        gram_own[0, index : index + 1] = inner(vectors[i][...], vectors[j][...])
     gram_own[0, len(PAIRS) : GRAM_ROWS] = jnp.zeros((GRAM_ROWS - len(PAIRS), 128), F32)
+
+    def apply_transposed(blocks, value):
+        return jnp.concatenate(
+            [jnp.sum(block * value, axis=0, keepdims=True) for block in blocks], axis=0
+        )
+
+    def step_transposed(value):
+        x = apply_transposed(diag_at[0], value[0]) + apply_transposed(outward[0], value[1])
+        return apply_transposed(pre_at[0], x) - SHIFT * value[0]
+
+    ends_at.append(ends_of(spare[0]))
+    turned_at = [
+        step_transposed([value, ends_of(vector[...], extracts[1])])
+        for value, vector in zip(ends_at, vectors)
+    ]
     for copy in copies:
         copy.wait_recv()
 
     joined = pieces(recvs_two, slice(8, 12))
     first = near_balances(recvs_two, gather)
     second = next_balances(first, joined, blocks, crosses, matches)
-    basis[3] = bulk[...] + at_ends(apply(in_blocks, first[2]))
-    advance(basis.at[3], bulk, image.at[3])
-    basis[4] = bulk[...] + at_ends(apply(in_blocks, second))
-    gram_rows(basis, 6, len(PAIRS))
-
-    partial = jnp.sum(gram_own[0], axis=1, keepdims=True)
+    added_one = apply(in_blocks, first[2])
+    added_two = apply(in_blocks, second)
+    put_one = at_depths(added_one)
+    put_two = at_depths(added_two)
+    moved = step_at_ends(put_one)
+    more = [ends_at[i] * added_one for i in range(3)]
+    more.append((2.0 * ends_at[3] + put_one[0]) * added_one)
+    more += [turned_at[i] * added_one + ends_at[i] * added_two for i in range(3)]
+    more.append(
+        (turned_at[3] + ends_at[4] + moved[0]) * added_one + (ends_at[3] + put_one[0]) * added_two
+    )
+    more.append(
+        (2.0 * turned_at[4] + step_transposed(moved)) * added_one
+        + (2.0 * (ends_at[4] + moved[0]) + put_two[0]) * added_two
+    )
+    more = [jnp.sum(value, axis=0, keepdims=True) for value in more]
+    empty = jnp.zeros((1, 128), F32)
+    more = [empty] * 6 + more + [empty] * (GRAM_ROWS - len(PAIRS))
+
+    sums = gram_own[0] + jnp.concatenate(more, axis=0)
+    partial = jnp.sum(sums, axis=1, keepdims=True)
     eye = iota((GRAM_ROWS, 128), 0) == iota((GRAM_ROWS, 128), 1)
     mine = row * columns + col
     gram_row[0] = jnp.sum(jnp.where(eye, partial, 0.0), axis=0, keepdims=True)
@@ -503,6 +540,12 @@
         return carry
 
     lax.fori_loop(0, others, tell, 0, unroll=5)
+    basis[3] = bulk[...] + at_ends(added_one)
+    for a in range(4):
+        value = precond[a, 0].astype(F32) * basis[3, 0]
+        for b in range(1, 4):
+            value = value + precond[a, b].astype(F32) * basis[3, b]
+        image[3, a] = value
     received = gram_all.at[0:others]
     pltpu.make_async_copy(received, received, all_recv).wait()
     total = jnp.sum(gram_all[...], axis=0)
@@ -537,7 +580,7 @@
         out_specs=pl.BlockSpec(memory_space=pltpu.VMEM),
         scratch_shapes=inputs
         + [
-            pltpu.VMEM((ITERS + 1, 4, pipes, slots), F32),
+            pltpu.VMEM((ITERS, 4, pipes, slots), F32),
             pltpu.VMEM((ITERS, 4, pipes, slots), F32),
             pltpu.VMEM((4, pipes, slots), F32),
             pltpu.VMEM((2, 4, pipes, slots), F32),

time: 29.9 us -> 29.6 us (0.990)
  Pallas kernels: 29.1 us -> 28.8 us
where the time goes in v6:
time: 29.6 us; the launch traced here: 29.5 us
  Pallas kernels  28.8 us (97%)
  local copies, waits for them, and re-layouts  0.66 us (2%)
    pallas_call x1, Pallas kernels, body(): pl.pallas_call(functools.partial(kernel, rows, columns), out_shape=pltpu....  28.8 us
    unnamed x1, local copies, waits for them, and re-layouts  0.66 us

profile of v6, /device:TPU:1, one launch (start us, length us, event | category | flops | bytes accessed | tf_op | source)
XLA Modules:
  0.0 29.5 jit_solution(6294390145688483396)
XLA Ops:
  0.0 28.8 %shard_map.91 = f32[4,32,256]{2,1,0:T(8,128)S(1)} custom-call(f32[4,32,256]{2,1,0:T(8,128)} %right_hbm.1, bf16[4,4,32,256]{3,2,1,0:T(8,128)(2,1)} %diag_hbm.1, bf16[4,4,32,256]{3,2,1,0:T(8,128)(2,1)} %lower_hbm.1, bf16[4,4,32,256]{3,2,1,0:T(8,128)(2,1)} %upper_hbm.1, bf16[4,4,32,256]{3,2,1,0:T(8,128)(2,1)} %precond_hbm.1, f32[2,4,4,32]{3,2,1,0:T(4,128)} %out_hbm_blocks.1, ...), custom_call_target="tpu_custom_call" | custom-call | tf_op jit(solution)/shard_map/pallas_call | solution.py:576
  28.9 0.7 %copy.11 = f32[4,32,256]{2,1,0:T(8,128)} copy(f32[4,32,256]{2,1,0:T(8,128)S(1)} %shard_map.91) | data formatting | bytes 262144

commit v7 on v6

--- a/solution.py
+++ b/solution.py
@@ -524,14 +524,14 @@
     eye = iota((GRAM_ROWS, 128), 0) == iota((GRAM_ROWS, 128), 1)
     mine = row * columns + col
     gram_row[0] = jnp.sum(jnp.where(eye, partial, 0.0), axis=0, keepdims=True)
-    gram_all[mine] = gram_row[0]
+    gram_all[pl.ds(mine, 1)] = gram_row[0]
     others = rows * columns - 1
 
     def tell(index, carry):
         target = index + jnp.where(index >= row * columns, 1, 0)
         pltpu.make_async_remote_copy(
             src_ref=gram_row.at[0],
-            dst_ref=gram_all.at[mine],
+            dst_ref=gram_all.at[pl.ds(mine, 1)],
             send_sem=all_send,
             recv_sem=all_recv,
             device_id=(target // columns, (col + target) % columns),
@@ -547,8 +547,11 @@
             value = value + precond[a, b].astype(F32) * basis[3, b]
         image[3, a] = value
     received = gram_all.at[0:others]
+    for copy in pending:
+        copy.wait_send()
+    pltpu.make_async_copy(received, received, all_send).wait()
     pltpu.make_async_copy(received, received, all_recv).wait()
-    total = jnp.sum(gram_all[...], axis=0)
+    total = jnp.sum(gram_all[...], axis=0, keepdims=True)
     splat = jnp.sum(jnp.where(eye, total, 0.0), axis=1, keepdims=True)
     splat = jnp.broadcast_to(splat, (GRAM_ROWS, 128))
     gram = {
@@ -562,9 +565,6 @@
             for k in range(1, ITERS):
                 value = value + coeffs[k] * image[k, a, :, lanes]
             result[a, :, lanes] = value
-    for copy in pending:
-        copy.wait_send()
-    pltpu.make_async_copy(received, received, all_send).wait()
 
 
 def body(rows, columns, right_side, diag, lower, upper, precond, jout, jin, junction, length):
@@ -592,7 +592,7 @@
             pltpu.VMEM((PIECES, 16, 128), F32),
             pltpu.VMEM((1, GRAM_ROWS, 128), F32),
             pltpu.VMEM((1, 1, 128), F32),
-            pltpu.VMEM((rows * columns, 1, 128), F32),
+            pltpu.VMEM((rows * columns, 128), F32),
             pltpu.SemaphoreType.DMA((len(operands),)),
             pltpu.SemaphoreType.DMA((2, PEERS)),
             pltpu.SemaphoreType.DMA((2, PEERS)),

time: 29.6 us -> 29.3 us (0.990)
  Pallas kernels: 28.8 us -> 28.5 us
    pallas_call x1, Pallas kernels: 28.8 us -> 28.5 us  [body(): pl.pallas_call(functools.partial(kernel, rows, columns), out_shape=pltpu....]
where the time goes in v7:
time: 29.3 us; the launch traced here: 29.2 us
  Pallas kernels  28.5 us (97%)
  local copies, waits for them, and re-layouts  0.66 us (2%)
    pallas_call x1, Pallas kernels, body(): pl.pallas_call(functools.partial(kernel, rows, columns), out_shape=pltpu....  28.5 us
    unnamed x1, local copies, waits for them, and re-layouts  0.66 us

profile of v7, /device:TPU:1, one launch (start us, length us, event | category | flops | bytes accessed | tf_op | source)
XLA Modules:
  0.0 29.2 jit_solution(13054741982028193224)
XLA Ops:
  0.0 28.5 %shard_map.91 = f32[4,32,256]{2,1,0:T(8,128)S(1)} custom-call(f32[4,32,256]{2,1,0:T(8,128)} %right_hbm.1, bf16[4,4,32,256]{3,2,1,0:T(8,128)(2,1)} %diag_hbm.1, bf16[4,4,32,256]{3,2,1,0:T(8,128)(2,1)} %lower_hbm.1, bf16[4,4,32,256]{3,2,1,0:T(8,128)(2,1)} %upper_hbm.1, bf16[4,4,32,256]{3,2,1,0:T(8,128)(2,1)} %precond_hbm.1, f32[2,4,4,32]{3,2,1,0:T(4,128)} %out_hbm_blocks.1, ...), custom_call_target="tpu_custom_call" | custom-call | tf_op jit(solution)/shard_map/pallas_call | solution.py:576
  28.6 0.7 %copy.11 = f32[4,32,256]{2,1,0:T(8,128)} copy(f32[4,32,256]{2,1,0:T(8,128)S(1)} %shard_map.91) | data formatting | bytes 262144

commit v8 on v7

--- a/solution.py
+++ b/solution.py
@@ -13,7 +13,8 @@
 FAR = 2 * SPAN
 PIECES = 2 * SPAN + 1
 PEERS = 2 * FAR + 1
-SHIFT = 1.0
+SCALE = 0.0625
+SHIFT = SCALE
 CHUNK = 16
 MESH = pl.DeviceIdType.MESH
 F32 = jnp.float32
@@ -227,7 +228,7 @@
         return [total[4 * a : 4 * a + 4] for a in range(4)]
 
     pre_blocks = jnp.concatenate([precond[a, b] for b in range(4) for a in range(4)], axis=0)
-    pre_ends = block_ends(pre_blocks, extract)
+    pre_ends = [SCALE * value for value in block_ends(pre_blocks, extract)]
     to_balance = [
         sum(out_blocks[a] * pre_ends[b][a : a + 1] for a in range(4)) for b in range(4)
     ]
@@ -314,6 +315,7 @@
                 total = precond[a, 0, part].astype(F32) * vec[0]
                 for b in range(1, 4):
                     total = total + precond[a, b, part].astype(F32) * vec[b]
+                total = SCALE * total
                 if picture is not None:
                     picture[a, part] = total
                 x.append(total)
@@ -389,7 +391,9 @@
         slot = jnp.where(is_first, depth, length_row - 1 - depth)
         slot = jnp.where(used & (length_row > depth), slot, -1)
         extracts.append((iota((256, 128), 0) == slot).astype(F32).astype(BF16))
-    pre_at = [pre_ends] + [block_ends(pre_blocks, extracts[d]) for d in (1, 2)]
+    pre_at = [pre_ends] + [
+        [SCALE * value for value in block_ends(pre_blocks, extracts[d])] for d in (1, 2)
+    ]
     diag_at = [block_ends(diag[...].reshape(512, 256), extracts[d]) for d in (0, 1)]
     lower_at = [block_ends(lower[...].reshape(512, 256), extracts[d]) for d in range(3)]
     upper_at = [block_ends(upper[...].reshape(512, 256), extracts[d]) for d in range(3)]
@@ -545,7 +549,7 @@
         value = precond[a, 0].astype(F32) * basis[3, 0]
         for b in range(1, 4):
             value = value + precond[a, b].astype(F32) * basis[3, b]
-        image[3, a] = value
+        image[3, a] = SCALE * value
     received = gram_all.at[0:others]
     for copy in pending:
         copy.wait_send()

time: 29.3 us -> 29.3 us (level)
  no operation moved by 1% of the time
where the time goes in v8:
time: 29.3 us; the launch traced here: 29.2 us
  Pallas kernels  28.6 us (98%)
  local copies, waits for them, and re-layouts  0.66 us (2%)
    pallas_call x1, Pallas kernels, body(): pl.pallas_call(functools.partial(kernel, rows, columns), out_shape=pltpu....  28.6 us
    unnamed x1, local copies, waits for them, and re-layouts  0.66 us

profile of v8, /device:TPU:1, one launch (start us, length us, event | category | flops | bytes accessed | tf_op | source)
XLA Modules:
  0.0 29.2 jit_solution(4873793516156879741)
XLA Ops:
  0.0 28.6 %shard_map.91 = f32[4,32,256]{2,1,0:T(8,128)S(1)} custom-call(f32[4,32,256]{2,1,0:T(8,128)} %right_hbm.1, bf16[4,4,32,256]{3,2,1,0:T(8,128)(2,1)} %diag_hbm.1, bf16[4,4,32,256]{3,2,1,0:T(8,128)(2,1)} %lower_hbm.1, bf16[4,4,32,256]{3,2,1,0:T(8,128)(2,1)} %upper_hbm.1, bf16[4,4,32,256]{3,2,1,0:T(8,128)(2,1)} %precond_hbm.1, f32[2,4,4,32]{3,2,1,0:T(4,128)} %out_hbm_blocks.1, ...), custom_call_target="tpu_custom_call" | custom-call | tf_op jit(solution)/shard_map/pallas_call | solution.py:580
  28.6 0.7 %copy.11 = f32[4,32,256]{2,1,0:T(8,128)} copy(f32[4,32,256]{2,1,0:T(8,128)S(1)} %shard_map.91) | data formatting | bytes 262144
